TPU v7x, 32 devices: a whole 2x2x4 slice. The times are simulated.
32 devices in a mesh: groups: 2 (over y), blk: 16 (over z, x, core).
Axes of the slice: x: 2, y: 2, z: 4, core: 2. Of those that a mesh axis runs over, the one named last changes fastest.
Arguments:
- image_embed: bfloat16 [4096, 1152], P(('groups', 'blk')), parts along dimension 0, may hold values from -6 to 6
- report_embed: bfloat16 [4096, 1152], P(('groups', 'blk')), parts along dimension 0, may hold values from -6 to 6
- image_study: int32 [4096], P(('groups', 'blk')), parts along dimension 0, may hold values from 0 to 1023, as said below
- report_study_index: int32 [4096], P(('groups', 'blk')), parts along dimension 0, may hold values from 0 to 1023, as said below
- logit_scale: float32 [2], P('groups'), parts along dimension 0, may hold values from 6 to 16
- logit_bias: float32 [2], P('groups'), parts along dimension 0, may hold values from -6 to -2
Outputs:
- loss: float32 [2], P('groups'), parts along dimension 0
- image_grad: float32 [4096, 1152], P(('groups', 'blk')), parts along dimension 0
- report_grad: float32 [4096, 1152], P(('groups', 'blk')), parts along dimension 0
There are 2 independent parts, one for each index of `groups`. A program takes and returns all parts, laid end to end along the dimension named above; each array names one. Nothing has to cross between parts.
Inputs may be any that keep to these rules, and one draw needn't show every extreme that they name: `image_study`: each study id names exactly two images; image i and report i belong to the same study for most i, and the reports hold the same ids as the images, each exactly twice. `report_study_index`: each study id names exactly two reports.
All inputs are finite; a program needn't handle non-finite values.
Results may differ from a plain program's by a relative error of at most 0.0003.
The roundings to bfloat16 on the way count: a program that leaves them out, or rounds other values in their place, can miss the bound.
Values may be sent and summed in bfloat16 or wider, within the bound.
A program may use at most 128 MiB of HBM per device.

v0:
```python
import math

import jax
import jax.numpy as jnp
from jax import lax
from jax.sharding import PartitionSpec as P


def shortened(value):

    def short(part):
        return part.astype(jnp.bfloat16) if part.dtype == jnp.float32 else part

    return jax.tree.map(short, value)


def from_partner(value, axis, stride):
    return lax.ppermute(value, axis, [(i, i ^ 1 << stride) for i in range(lax.axis_size(axis))])


def unit_rows(embed):
    values = embed.astype(jnp.float32)
    norm = jnp.sqrt(jnp.sum(values * values, axis=1, keepdims=True) + 1e-06)
    unit = values / norm
    return (norm, unit, unit.astype(jnp.bfloat16))


def finish(unit_grad, unit, norm):
    return (unit_grad - unit * jnp.sum(unit * unit_grad, axis=1, keepdims=True)) / norm


def placed(upper, mine, theirs):
    return jnp.where(
        upper, jnp.concatenate([theirs, mine], axis=0), jnp.concatenate([mine, theirs], axis=0)
    )


def body(image_embed, report_embed, image_study, report_study_index, logit_scale, logit_bias):
    image_norm, image_unit, image_send = unit_rows(image_embed)
    report_norm, report_unit, report_send = unit_rows(report_embed)
    scale = logit_scale[0]
    bias = logit_bias[0]
    total_bits = lax.axis_size("blk").bit_length() - 1
    image_count = (total_bits + 1) // 2
    report_list = list(range(total_bits - image_count))
    image_list = list(range(total_bits - image_count, total_bits))
    block_position = lax.axis_index("blk")
    images, image_ids = (image_send, image_study)
    for bit in image_list:
        upper = block_position >> bit & 1 == 1
        other_rows, other_ids = (
            from_partner(images, "blk", bit),
            from_partner(shortened(image_ids), "blk", bit).astype(image_ids.dtype),
        )
        images = placed(upper, images, other_rows)
        image_ids = placed(upper, image_ids, other_ids)
    reports, report_index_list = (report_send, report_study_index)
    for bit in report_list:
        upper = block_position >> bit & 1 == 1
        other_rows, other_ids = (
            from_partner(reports, "blk", bit),
            from_partner(shortened(report_index_list), "blk", bit).astype(report_index_list.dtype),
        )
        reports = placed(upper, reports, other_rows)
        report_index_list = placed(upper, report_index_list, other_ids)
    image_total = images.shape[0]
    width = images.shape[1]
    block_rows = math.gcd(image_total, 512)
    block_count = image_total // block_rows
    image_blocks = images.reshape(block_count, block_rows, width)
    id_blocks = image_ids.reshape(block_count, block_rows)

    def step(carry, input_arrays):
        report_acc, loss_acc = carry
        block_slice, study_labels = input_arrays
        logits = (
            scale
            * lax.dot_general(
                block_slice, reports, (((1,), (1,)), ((), ())), preferred_element_type=jnp.float32
            )
            + bias
        )
        pair_sign = jnp.where(
            study_labels[:, None] == report_index_list[None, :], 1.0, -1.0
        ).astype(jnp.float32)
        loss_acc = loss_acc - jnp.sum(jax.nn.log_sigmoid(pair_sign * logits))
        coeff = (-pair_sign * jax.nn.sigmoid(-pair_sign * logits)).astype(jnp.bfloat16)
        image_part = scale * jnp.dot(coeff, reports, preferred_element_type=jnp.float32)
        report_acc = report_acc + scale * lax.dot_general(
            coeff, block_slice, (((0,), (0,)), ((), ())), preferred_element_type=jnp.float32
        )
        return ((report_acc, loss_acc), image_part)

    start = (jnp.zeros((reports.shape[0], width), jnp.float32), jnp.zeros((), jnp.float32))
    (report_part, loss_part), image_parts = lax.scan(step, start, (image_blocks, id_blocks))
    image_part = image_parts.reshape(image_total, width)
    for bit in reversed(image_list):
        upper = block_position >> bit & 1 == 1
        half = image_part.shape[0] // 2
        keep = jnp.where(upper, image_part[half:], image_part[:half])
        give = jnp.where(upper, image_part[:half], image_part[half:])
        image_part = keep + from_partner(give, "blk", bit)
    for bit in reversed(report_list):
        upper = block_position >> bit & 1 == 1
        half = report_part.shape[0] // 2
        keep = jnp.where(upper, report_part[half:], report_part[:half])
        give = jnp.where(upper, report_part[:half], report_part[half:])
        report_part = keep + from_partner(give, "blk", bit)
    total = lax.psum(loss_part, "blk")
    pair_count = image_embed.shape[0] * lax.axis_size("blk")
    loss = (total / pair_count).reshape(1)
    image_grad = finish(image_part, image_unit, image_norm)
    report_grad = finish(report_part, report_unit, report_norm)
    return (loss, image_grad, report_grad)


def solution(mesh):
    return jax.shard_map(
        body,
        mesh=mesh,
        in_specs=(
            P(("groups", "blk"), None),
            P(("groups", "blk"), None),
            P(("groups", "blk")),
            P(("groups", "blk")),
            P("groups"),
            P("groups"),
        ),
        out_specs=(P("groups"), P(("groups", "blk"), None), P(("groups", "blk"), None)),
        check_vma=False,
    )
```

profile of v0, /device:TPU:0, one launch (start us, length us, event | category | flops | bytes accessed | tf_op | source)
XLA Modules:
  0.0 141.5 jit_solution(17538157425090612572)
XLA Ops:
  0.6 0.0 copy-start.1
  0.6 1.1 fusion.11
  1.8 1.1 fusion.16
  2.9 0.5 collective-permute-start.6
  3.4 1.1 fusion.10
  4.5 0.1 fusion.15
  4.7 2.7 %collective-permute-start.4 = (bf16[128,1152]{1,0:T(8,128)(2,1)S(1)}, bf16[128,1152]{1,0:T(8,128)(2,1)S(1)}, u32[]{:S(2)}, u32[]{:S(2)}) collective-permute-start(bf16[128,1152]{1,0:T(8,128)(2,1)S(1)} %fusion.15), channel_id=1, source_target_pairs={{0,4},{1,5},{2,6},{3,7},{4,0},{5,1},{6,2},{7,3},{8,12},{9,13},{10,... | collective-permute-start | bytes 884744 | tf_op jit(solution)/shard_map/ppermute | solution.py:18
  7.3 0.0 collective-permute-done.6
  7.3 0.1 maximum_select_fusion.3
  7.4 1.6 %collective-permute-start.7 = (bf16[256,1152]{1,0:T(8,128)(2,1)S(1)}, bf16[256,1152]{1,0:T(8,128)(2,1)}, u32[]{:S(2)}, u32[]{:S(2)}) collective-permute-start(bf16[256,1152]{1,0:T(8,128)(2,1)S(1)} %maximum_select_fusion.3), channel_id=1, source_target_pairs={{0,2},{1,3},{2,0},{3,1},{4,6},{5,7},{6,4},{7,5},{8,10},{9,11},{10,... | collective-permute-start | bytes 1769480 | tf_op jit(solution)/shard_map/ppermute | solution.py:18
  9.0 6.0 %collective-permute-done.4 = bf16[128,1152]{1,0:T(8,128)(2,1)S(1)} collective-permute-done((bf16[128,1152]{1,0:T(8,128)(2,1)S(1)}, bf16[128,1152]{1,0:T(8,128)(2,1)S(1)}, u32[]{:S(2)}, u32[]{:S(2)}) %collective-permute-start.4) | collective-permute-done | bytes 294944 | tf_op jit(solution)/shard_map/ppermute | solution.py:18
  15.0 0.1 maximum_select_fusion.2
  15.1 2.8 %collective-permute-start.5 = (bf16[256,1152]{1,0:T(8,128)(2,1)S(1)}, bf16[256,1152]{1,0:T(8,128)(2,1)S(1)}, u32[]{:S(2)}, u32[]{:S(2)}) collective-permute-start(bf16[256,1152]{1,0:T(8,128)(2,1)S(1)} %maximum_select_fusion.2), channel_id=1, source_target_pairs={{0,8},{1,9},{2,10},{3,11},{4,12},{5,13},{6,14},{7,15},{8,0},{9,1},... | collective-permute-start | bytes 1769480 | tf_op jit(solution)/shard_map/ppermute | solution.py:18
  17.9 0.0 collective-permute-start.2
  17.9 1.6 %collective-permute-start = (s32[128]{0:T(128)S(1)}, s32[128]{0:T(128)S(1)}, u32[]{:S(2)}, u32[]{:S(2)}) collective-permute-start(s32[128]{0:T(128)S(1)} %copy-done.4), channel_id=1, source_target_pairs={{0,4},{1,5},{2,6},{3,7},{4,0},{5,1},{6,2},{7,3},{8,12},{9,13},{10,... | collective-permute-start | bytes 1544 | tf_op jit(solution)/shard_map/ppermute | solution.py:18
  20.9 0.0 collective-permute-done.2
  20.9 1.6 %collective-permute-start.3 = (s32[256]{0:T(256)S(1)}, s32[256]{0:T(256)S(1)}, u32[]{:S(2)}, u32[]{:S(2)}) collective-permute-start(s32[256]{0:T(256)S(1)} %add_select_fusion.3), channel_id=1, source_target_pairs={{0,2},{1,3},{2,0},{3,1},{4,6},{5,7},{6,4},{7,5},{8,10},{9,11},{10,... | collective-permute-start | bytes 3080 | tf_op jit(solution)/shard_map/ppermute | solution.py:18
  22.5 8.1 %collective-permute-done = s32[128]{0:T(128)S(1)} collective-permute-done((s32[128]{0:T(128)S(1)}, s32[128]{0:T(128)S(1)}, u32[]{:S(2)}, u32[]{:S(2)}) %collective-permute-start) | collective-permute-done | bytes 544 | tf_op jit(solution)/shard_map/ppermute | solution.py:18
  30.6 2.3 %collective-permute-start.1 = (s32[256]{0:T(256)S(1)}, s32[256]{0:T(256)S(1)}, u32[]{:S(2)}, u32[]{:S(2)}) collective-permute-start(s32[256]{0:T(256)S(1)} %add_select_fusion.2), channel_id=1, source_target_pairs={{0,8},{1,9},{2,10},{3,11},{4,12},{5,13},{6,14},{7,15},{8,0},{9,1},... | collective-permute-start | bytes 3080 | tf_op jit(solution)/shard_map/ppermute | solution.py:18
  32.9 0.0 collective-permute-done.3
  32.9 11.1 %collective-permute-done.1 = s32[256]{0:T(256)S(1)} collective-permute-done((s32[256]{0:T(256)S(1)}, s32[256]{0:T(256)S(1)}, u32[]{:S(2)}, u32[]{:S(2)}) %collective-permute-start.1) | collective-permute-done | bytes 1056 | tf_op jit(solution)/shard_map/ppermute | solution.py:18
  44.1 0.0 collective-permute-done.7
  44.1 0.0 collective-permute-done.5
  44.1 0.0 copy-start.5
  44.1 3.8 %fusion.8 = (f32[]{:T(128)}, f32[512,512]{1,0:T(8,128)S(1)}) fusion(s32[512]{0:T(512)S(1)} %add_select_fusion.1, s32[512]{0:T(512)S(1)} %add_select_fusion, f32[]{:T(128)} %bitcast.6, bf16[256,1152]{1,0:T(8,128)(2,1)S(1)} %maximum_select_fusion.3, bf16[256,1152]{1,0:T(8,128)(2,1)} %collective-permute-done.7, pred[]{:T(512)S(6)} %eq.39, ...), kind=kOutput, calls=%fused_computation.20 | convolution fusion | flops 618004480 | bytes 3411982 | tf_op jit(solution)/shard_map/while/body/eval_jaxpr/dot_general | solution.py:78
  47.8 2.4 %convolution_multiply_fusion.1 = f32[512,1152]{1,0:T(8,128)S(1)} fusion(f32[]{:T(128)} %bitcast.4, bf16[256,1152]{1,0:T(8,128)(2,1)S(1)} %maximum_select_fusion.3, bf16[256,1152]{1,0:T(8,128)(2,1)} %collective-permute-done.7, pred[]{:T(512)S(6)} %eq.39, f32[512,512]{1,0:T(8,128)S(1)} %get-tuple-element.28, s32[512]{0:T(512)S(1)} %add_select_fusion.1, ...), kind=kOutput, calls=%fused_computation.1 | convolution fusion | flops 612237312 | bytes 4591621 | tf_op jit(solution)/shard_map/while/body/eval_jaxpr/dot_general | solution.py:88
  50.3 0.0 copy-start.6
  50.3 1.1 slice_select_fusion.1
  51.4 0.6 copy-done
  52.1 0.0 collective-permute-start.8
  52.1 1.3 convolution_multiply_fusion
  53.4 1.1 slice_select_fusion
  54.5 1.5 %collective-permute-start.10 = (f32[256,1152]{1,0:T(8,128)}, f32[256,1152]{1,0:T(8,128)}, u32[]{:S(2)}, u32[]{:S(2)}) collective-permute-start(f32[256,1152]{1,0:T(8,128)} %slice_select_fusion), channel_id=1, source_target_pairs={{0,2},{1,3},{2,0},{3,1},{4,6},{5,7},{6,4},{7,5},{8,10},{9,11},{10,... | collective-permute-start | bytes 3538952 | tf_op jit(solution)/shard_map/ppermute | solution.py:18
  56.7 57.0 %psum.7 = f32[]{:T(128)} all-reduce(f32[]{:T(128)S(6)} %sub.10), channel_id=1, replica_groups=mesh['groups'=2,'blk'=16] {'blk'}, use_global_device_ids=true, to_apply=%region_3.4 | all-reduce | flops 1 | bytes 8 | tf_op jit(solution)/shard_map/psum | solution.py:109
  114.3 0.0 collective-permute-done.8
  114.4 2.2 %select_add_fusion.1 = f32[256,1152]{1,0:T(8,128)S(1)} fusion(f32[256,1152]{1,0:T(8,128)} %collective-permute-done.8, f32[512,1152]{1,0:T(8,128)} %copy-done, pred[]{:T(512)S(6)} %eq.36), kind=kLoop, calls=%fused_computation.12 | loop fusion | flops 589824 | bytes 4718593 | tf_op jit(solution)/shard_map/add | solution.py:102
  116.5 0.1 slice_select_fusion.3
  116.6 7.6 %collective-permute-start.9 = (f32[128,1152]{1,0:T(8,128)S(1)}, f32[128,1152]{1,0:T(8,128)S(1)}, u32[]{:S(2)}, u32[]{:S(2)}) collective-permute-start(f32[128,1152]{1,0:T(8,128)S(1)} %slice_select_fusion.3), channel_id=1, source_target_pairs={{0,4},{1,5},{2,6},{3,7},{4,0},{5,1},{6,2},{7,3},{8,12},{9,13},{10,... | collective-permute-start | bytes 1769480 | tf_op jit(solution)/shard_map/ppermute | solution.py:18
  124.1 0.0 collective-permute-done.10
  124.1 1.4 %select_add_fusion = f32[256,1152]{1,0:T(8,128)S(1)} fusion(f32[256,1152]{1,0:T(8,128)} %collective-permute-done.10, f32[512,1152]{1,0:T(8,128)S(1)} %convolution_multiply_fusion, pred[]{:T(512)S(6)} %eq.39), kind=kLoop, calls=%fused_computation.11 | loop fusion | flops 589824 | bytes 4718593 | tf_op jit(solution)/shard_map/add | solution.py:108
  125.6 0.1 slice_select_fusion.2
  125.7 0.1 collective-permute-start.11
  125.7 12.0 %collective-permute-done.9 = f32[128,1152]{1,0:T(8,128)S(1)} collective-permute-done((f32[128,1152]{1,0:T(8,128)S(1)}, f32[128,1152]{1,0:T(8,128)S(1)}, u32[]{:S(2)}, u32[]{:S(2)}) %collective-permute-start.9) | collective-permute-done | bytes 589856 | tf_op jit(solution)/shard_map/ppermute | solution.py:18
  137.7 0.3 multiply_reduce_fusion.1
  138.0 1.0 subtract_divide_fusion.1
  139.0 0.0 collective-permute-done.11
  139.0 0.3 multiply_reduce_fusion
  139.3 1.0 subtract_divide_fusion
  (16 shorter events, 0.1 us)
Async XLA Ops:
  0.6 3.9 %copy-start.1 = (bf16[128,1152]{1,0:T(8,128)(2,1)S(1)}, bf16[128,1152]{1,0:T(8,128)(2,1)}, u32[]{:S(2)}) copy-start(bf16[128,1152]{1,0:T(8,128)(2,1)} %param.6) | copy-start | bytes 884740
  2.9 4.4 %collective-permute-start.6 = (bf16[128,1152]{1,0:T(8,128)(2,1)S(1)}, bf16[128,1152]{1,0:T(8,128)(2,1)S(1)}, u32[]{:S(2)}, u32[]{:S(2)}) collective-permute-start(bf16[128,1152]{1,0:T(8,128)(2,1)S(1)} %fusion.16), channel_id=1, source_target_pairs={{0,1},{1,0},{2,3},{3,2},{4,5},{5,4},{6,7},{7,6},{8,9},{9,8},{10,11... | collective-permute-start | bytes 884744 | tf_op jit(solution)/shard_map/ppermute | solution.py:18
  4.7 10.3 %collective-permute-start.4 = (bf16[128,1152]{1,0:T(8,128)(2,1)S(1)}, bf16[128,1152]{1,0:T(8,128)(2,1)S(1)}, u32[]{:S(2)}, u32[]{:S(2)}) collective-permute-start(bf16[128,1152]{1,0:T(8,128)(2,1)S(1)} %fusion.15), channel_id=1, source_target_pairs={{0,4},{1,5},{2,6},{3,7},{4,0},{5,1},{6,2},{7,3},{8,12},{9,13},{10,... | collective-permute-start | bytes 884744 | tf_op jit(solution)/shard_map/ppermute | solution.py:18
  7.3 10.6 %copy-start.3 = (s32[128]{0:T(128)S(1)}, s32[128]{0:T(128)}, u32[]{:S(2)}) copy-start(s32[128]{0:T(128)} %param.9) | copy-start | bytes 1540
  7.3 10.6 %copy-start.4 = (s32[128]{0:T(128)S(1)}, s32[128]{0:T(128)}, u32[]{:S(2)}) copy-start(s32[128]{0:T(128)} %param.8) | copy-start | bytes 1540
  7.4 36.6 %collective-permute-start.7 = (bf16[256,1152]{1,0:T(8,128)(2,1)S(1)}, bf16[256,1152]{1,0:T(8,128)(2,1)}, u32[]{:S(2)}, u32[]{:S(2)}) collective-permute-start(bf16[256,1152]{1,0:T(8,128)(2,1)S(1)} %maximum_select_fusion.3), channel_id=1, source_target_pairs={{0,2},{1,3},{2,0},{3,1},{4,6},{5,7},{6,4},{7,5},{8,10},{9,11},{10,... | collective-permute-start | bytes 1769480 | tf_op jit(solution)/shard_map/ppermute | solution.py:18
  15.1 29.0 %collective-permute-start.5 = (bf16[256,1152]{1,0:T(8,128)(2,1)S(1)}, bf16[256,1152]{1,0:T(8,128)(2,1)S(1)}, u32[]{:S(2)}, u32[]{:S(2)}) collective-permute-start(bf16[256,1152]{1,0:T(8,128)(2,1)S(1)} %maximum_select_fusion.2), channel_id=1, source_target_pairs={{0,8},{1,9},{2,10},{3,11},{4,12},{5,13},{6,14},{7,15},{8,0},{9,1},... | collective-permute-start | bytes 1769480 | tf_op jit(solution)/shard_map/ppermute | solution.py:18
  17.9 3.0 %collective-permute-start.2 = (s32[128]{0:T(128)S(1)}, s32[128]{0:T(128)S(1)}, u32[]{:S(2)}, u32[]{:S(2)}) collective-permute-start(s32[128]{0:T(128)S(1)} %copy-done.3), channel_id=1, source_target_pairs={{0,1},{1,0},{2,3},{3,2},{4,5},{5,4},{6,7},{7,6},{8,9},{9,8},{10,11... | collective-permute-start | bytes 1544 | tf_op jit(solution)/shard_map/ppermute | solution.py:18
  17.9 12.6 %collective-permute-start = (s32[128]{0:T(128)S(1)}, s32[128]{0:T(128)S(1)}, u32[]{:S(2)}, u32[]{:S(2)}) collective-permute-start(s32[128]{0:T(128)S(1)} %copy-done.4), channel_id=1, source_target_pairs={{0,4},{1,5},{2,6},{3,7},{4,0},{5,1},{6,2},{7,3},{8,12},{9,13},{10,... | collective-permute-start | bytes 1544 | tf_op jit(solution)/shard_map/ppermute | solution.py:18
  20.9 12.0 %collective-permute-start.3 = (s32[256]{0:T(256)S(1)}, s32[256]{0:T(256)S(1)}, u32[]{:S(2)}, u32[]{:S(2)}) collective-permute-start(s32[256]{0:T(256)S(1)} %add_select_fusion.3), channel_id=1, source_target_pairs={{0,2},{1,3},{2,0},{3,1},{4,6},{5,7},{6,4},{7,5},{8,10},{9,11},{10,... | collective-permute-start | bytes 3080 | tf_op jit(solution)/shard_map/ppermute | solution.py:18
  30.6 13.5 %collective-permute-start.1 = (s32[256]{0:T(256)S(1)}, s32[256]{0:T(256)S(1)}, u32[]{:S(2)}, u32[]{:S(2)}) collective-permute-start(s32[256]{0:T(256)S(1)} %add_select_fusion.2), channel_id=1, source_target_pairs={{0,8},{1,9},{2,10},{3,11},{4,12},{5,13},{6,14},{7,15},{8,0},{9,1},... | collective-permute-start | bytes 3080 | tf_op jit(solution)/shard_map/ppermute | solution.py:18
  44.1 3.8 %copy-start.5 = (bf16[256,1152]{1,0:T(8,128)(2,1)}, bf16[256,1152]{1,0:T(8,128)(2,1)S(1)}, u32[]{:S(2)}) copy-start(bf16[256,1152]{1,0:T(8,128)(2,1)S(1)} %collective-permute-done.5) | copy-start | bytes 1769476
  50.3 1.8 %copy-start = (f32[512,1152]{1,0:T(8,128)}, f32[512,1152]{1,0:T(8,128)S(1)}, u32[]{:S(2)}) copy-start(f32[512,1152]{1,0:T(8,128)S(1)} %convolution_multiply_fusion.1) | copy-start | bytes 7077892
  50.3 1.8 %copy-start.6 = (bf16[256,1152]{1,0:T(8,128)(2,1)S(1)}, bf16[256,1152]{1,0:T(8,128)(2,1)}, u32[]{:S(2)}) copy-start(bf16[256,1152]{1,0:T(8,128)(2,1)} %copy-done.5) | copy-start | bytes 1769476
  52.1 62.3 %collective-permute-start.8 = (f32[256,1152]{1,0:T(8,128)}, f32[256,1152]{1,0:T(8,128)}, u32[]{:S(2)}, u32[]{:S(2)}) collective-permute-start(f32[256,1152]{1,0:T(8,128)} %slice_select_fusion.1), channel_id=1, source_target_pairs={{0,8},{1,9},{2,10},{3,11},{4,12},{5,13},{6,14},{7,15},{8,0},{9,1},... | collective-permute-start | bytes 3538952 | tf_op jit(solution)/shard_map/ppermute | solution.py:18
  54.5 69.6 %collective-permute-start.10 = (f32[256,1152]{1,0:T(8,128)}, f32[256,1152]{1,0:T(8,128)}, u32[]{:S(2)}, u32[]{:S(2)}) collective-permute-start(f32[256,1152]{1,0:T(8,128)} %slice_select_fusion), channel_id=1, source_target_pairs={{0,2},{1,3},{2,0},{3,1},{4,6},{5,7},{6,4},{7,5},{8,10},{9,11},{10,... | collective-permute-start | bytes 3538952 | tf_op jit(solution)/shard_map/ppermute | solution.py:18
  116.6 21.1 %collective-permute-start.9 = (f32[128,1152]{1,0:T(8,128)S(1)}, f32[128,1152]{1,0:T(8,128)S(1)}, u32[]{:S(2)}, u32[]{:S(2)}) collective-permute-start(f32[128,1152]{1,0:T(8,128)S(1)} %slice_select_fusion.3), channel_id=1, source_target_pairs={{0,4},{1,5},{2,6},{3,7},{4,0},{5,1},{6,2},{7,3},{8,12},{9,13},{10,... | collective-permute-start | bytes 1769480 | tf_op jit(solution)/shard_map/ppermute | solution.py:18
  125.7 13.4 %collective-permute-start.11 = (f32[128,1152]{1,0:T(8,128)S(1)}, f32[128,1152]{1,0:T(8,128)S(1)}, u32[]{:S(2)}, u32[]{:S(2)}) collective-permute-start(f32[128,1152]{1,0:T(8,128)S(1)} %slice_select_fusion.2), channel_id=1, source_target_pairs={{0,1},{1,0},{2,3},{3,2},{4,5},{5,4},{6,7},{7,6},{8,9},{9,8},{10,11... | collective-permute-start | bytes 1769480 | tf_op jit(solution)/shard_map/ppermute | solution.py:18
  138.0 1.0 copy-start.2
where the time goes:
time: 142 us; the launch traced here: 141 us
  blocking collectives  57 us (40%)
  waiting for transfers between devices  37.3 us (26%)
  starting transfers between devices  22.1 us (16%)
  other arithmetic  12.3 us (9%)
  matrix products  7.47 us (5%)
  between operations  4.57 us (3%)
    psum x1, blocking collectives, body(): total = lax.psum(loss_part, 'blk')  57 us
    ppermute x12, waiting for transfers between devices, from_partner(): lax.ppermute(value, axis, [(i, i ^ 1 << stride) for i in range(lax.axis_s...  37.3 us
    ppermute x12, starting transfers between devices, from_partner(): lax.ppermute(value, axis, [(i, i ^ 1 << stride) for i in range(lax.axis_s...  22.1 us
    dot_general x1, matrix products, step(): lax.dot_general(block_slice, reports, (((1,), (1,)), ((), ())), preferred...  3.75 us
  transfers between devices with their start and end apart: 12, of which 4 were waited for; matrix products, arithmetic and copies ran while one was open for 6% of the time, Pallas kernels for 0%

commit v1 on v0

--- a/solution.py
+++ b/solution.py
@@ -3,6 +3,8 @@
 import jax
 import jax.numpy as jnp
 from jax import lax
+from jax.experimental import pallas as pl
+from jax.experimental.pallas import tpu as pltpu
 from jax.sharding import PartitionSpec as P
 
 
@@ -114,9 +116,232 @@
     return (loss, image_grad, report_grad)
 
 
+CORE, ACROSS, NEAR, FAR = (1, 2, 4, 8)
+MESH_ID = pl.DeviceIdType.MESH
+
+
+def tile_kernel(
+    image_ref, report_ref, image_id_ref, report_id_ref, scale_ref, bias_ref,
+    loss_ref, image_grad_ref, report_grad_ref,
+    images, reports, image_ids, report_ids, coeffs, image_part, report_part,
+    core_in, far_in, across_in, near_in, far_out, near_out, loss_out, loss_in,
+    send_sem, recv_sem,
+):
+    group = lax.axis_index("groups")
+    me = lax.axis_index("blk")
+    rows = image_ref.shape[0]
+
+    def partner(bit):
+        low = lax.rem(lax.div(me, bit), 2)
+        return (group, me + bit - 2 * bit * low)
+
+    def send(number, source, target, bit):
+        copy = pltpu.make_async_remote_copy(
+            src_ref=source,
+            dst_ref=target,
+            send_sem=send_sem.at[number],
+            recv_sem=recv_sem.at[number],
+            device_id=partner(bit),
+            device_id_type=MESH_ID,
+        )
+        copy.start()
+        return copy
+
+    barrier = pltpu.get_barrier_semaphore()
+    for bit in (CORE, ACROSS, NEAR, FAR):
+        pl.semaphore_signal(barrier, inc=1, device_id=partner(bit), device_id_type=MESH_ID)
+
+    def normalised(ref):
+        values = ref[...].astype(jnp.float32)
+        norm = jnp.sqrt(jnp.sum(values * values, axis=1, keepdims=True) + 1e-06)
+        return (norm, values / norm)
+
+    reports[0] = normalised(report_ref)[1].astype(jnp.bfloat16)
+    images[0] = normalised(image_ref)[1].astype(jnp.bfloat16)
+    image_ids[0] = image_id_ref[...]
+    report_ids[0] = report_id_ref[...]
+    pl.semaphore_wait(barrier, 4)
+
+    report_near = send(0, reports.at[0], reports.at[2], NEAR)
+    report_near_id = send(1, report_ids.at[0], report_ids.at[2], NEAR)
+    report_across = send(2, reports.at[0], reports.at[1], ACROSS)
+    report_across_id = send(3, report_ids.at[0], report_ids.at[1], ACROSS)
+    image_far = send(4, images.at[0], images.at[2], FAR)
+    image_far_id = send(5, image_ids.at[0], image_ids.at[2], FAR)
+    image_core = send(6, images.at[0], images.at[1], CORE)
+    image_core_id = send(7, image_ids.at[0], image_ids.at[1], CORE)
+
+    scale = scale_ref[0]
+    bias = bias_ref[0]
+
+    def tile(i, j):
+        logits = (
+            scale
+            * lax.dot_general(
+                images[i], reports[j], (((1,), (1,)), ((), ())), preferred_element_type=jnp.float32
+            )
+            + bias
+        )
+        across = jnp.broadcast_to(report_ids[j, 0:1, :], (rows, rows))
+        down = jnp.broadcast_to(image_ids[i, 0:1, :], (rows, rows)).T
+        sign = jnp.where(across == down, 1.0, -1.0).astype(jnp.float32)
+        signed = sign * logits
+        weight = jnp.exp(-jnp.abs(signed))
+        negative = jnp.where(signed >= 0, weight, 1.0) / (1.0 + weight)
+        coeffs[i, :, j * rows : (j + 1) * rows] = (-sign * negative).astype(jnp.bfloat16)
+        return jnp.maximum(-signed, 0.0) + jnp.log1p(weight)
+
+    image_core.wait()
+    image_core_id.wait()
+    total = tile(0, 0) + tile(1, 0)
+    report_near.wait()
+    report_near_id.wait()
+    report_diag = send(8, reports.at[2], reports.at[3], ACROSS)
+    report_diag_id = send(9, report_ids.at[2], report_ids.at[3], ACROSS)
+    total += tile(0, 2) + tile(1, 2)
+    report_across.wait()
+    report_across_id.wait()
+    total += tile(0, 1) + tile(1, 1)
+    image_far.wait()
+    image_far_id.wait()
+    image_diag = send(10, images.at[2], images.at[3], CORE)
+    image_diag_id = send(11, image_ids.at[2], image_ids.at[3], CORE)
+    total += tile(2, 0) + tile(2, 1) + tile(2, 2)
+    image_diag.wait()
+    image_diag_id.wait()
+    total += tile(3, 0) + tile(3, 1) + tile(3, 2)
+    report_diag.wait()
+    report_diag_id.wait()
+    for i in range(4):
+        total += tile(i, 3)
+
+    def image_sum(i):
+        out = None
+        for j in range(4):
+            term = jnp.dot(
+                coeffs[i, :, j * rows : (j + 1) * rows], reports[j], preferred_element_type=jnp.float32
+            )
+            out = term if out is None else out + term
+        return scale * out
+
+    def report_sum(j):
+        out = None
+        for i in range(4):
+            term = lax.dot_general(
+                coeffs[i, :, j * rows : (j + 1) * rows],
+                images[i],
+                (((0,), (0,)), ((), ())),
+                preferred_element_type=jnp.float32,
+            )
+            out = term if out is None else out + term
+        return scale * out
+
+    report_part[0] = report_sum(3)
+    across_first = send(12, report_part.at[0], across_in.at[0], ACROSS)
+    image_part[0] = image_sum(3)
+    core_first = send(13, image_part.at[0], core_in.at[0], CORE)
+    far_sum = image_sum(2)
+    core_first.wait_recv()
+    far_out[...] = far_sum + core_in[0]
+    far_send = send(14, far_out, far_in, FAR)
+    report_part[1] = report_sum(1)
+    across_second = send(15, report_part.at[1], across_in.at[1], ACROSS)
+    image_part[1] = image_sum(1)
+    core_second = send(16, image_part.at[1], core_in.at[1], CORE)
+    near_sum = report_sum(2)
+
+    loss_out[0] = jnp.sum(total.reshape(rows // 8, 8, rows), axis=0)
+    loss_copies = []
+    for step, bit in enumerate((CORE, ACROSS, NEAR, FAR)):
+        copy = send(18 + step, loss_out.at[step], loss_in.at[step], bit)
+        if step == 0:
+            own_image = image_sum(0)
+        elif step == 1:
+            own_report = report_sum(0)
+        copy.wait()
+        if step < 3:
+            loss_out[step + 1] = loss_out[step] + loss_in[step]
+        else:
+            whole = loss_out[step] + loss_in[step]
+    pairs = rows * lax.axis_size("blk")
+    loss_ref[...] = jnp.full(loss_ref.shape, jnp.sum(whole) / pairs, jnp.float32)
+
+    across_first.wait_recv()
+    near_out[...] = near_sum + across_in[0]
+    near_send = send(17, near_out, near_in, NEAR)
+
+    def finish(ref, unit_grad):
+        norm, unit = normalised(ref)
+        return (unit_grad - unit * jnp.sum(unit * unit_grad, axis=1, keepdims=True)) / norm
+
+    core_second.wait_recv()
+    own_image += core_in[1]
+    far_send.wait()
+    image_grad_ref[...] = finish(image_ref, own_image + far_in[...])
+    across_second.wait_recv()
+    own_report += across_in[1]
+    near_send.wait()
+    report_grad_ref[...] = finish(report_ref, own_report + near_in[...])
+    across_first.wait_send()
+    across_second.wait_send()
+    core_first.wait_send()
+    core_second.wait_send()
+
+
+def kernel_body(image_embed, report_embed, image_study, report_study_index, logit_scale, logit_bias):
+    rows, width = image_embed.shape
+    f32 = jnp.float32
+
+    def id_rows(ids):
+        return jnp.broadcast_to(ids[None, :], (8, rows))
+
+    vmem = pl.BlockSpec(memory_space=pltpu.VMEM)
+    smem = pl.BlockSpec(memory_space=pltpu.SMEM)
+    loss, image_grad, report_grad = pl.pallas_call(
+        tile_kernel,
+        out_shape=(
+            jax.ShapeDtypeStruct((8, 128), f32),
+            jax.ShapeDtypeStruct((rows, width), f32),
+            jax.ShapeDtypeStruct((rows, width), f32),
+        ),
+        in_specs=[vmem, vmem, vmem, vmem, smem, smem],
+        out_specs=(vmem, vmem, vmem),
+        scratch_shapes=[
+            pltpu.VMEM((4, rows, width), jnp.bfloat16),
+            pltpu.VMEM((4, rows, width), jnp.bfloat16),
+            pltpu.VMEM((4, 8, rows), jnp.int32),
+            pltpu.VMEM((4, 8, rows), jnp.int32),
+            pltpu.VMEM((4, rows, 4 * rows), jnp.bfloat16),
+            pltpu.VMEM((2, rows, width), f32),
+            pltpu.VMEM((2, rows, width), f32),
+            pltpu.VMEM((2, rows, width), f32),
+            pltpu.VMEM((rows, width), f32),
+            pltpu.VMEM((2, rows, width), f32),
+            pltpu.VMEM((rows, width), f32),
+            pltpu.VMEM((rows, width), f32),
+            pltpu.VMEM((rows, width), f32),
+            pltpu.VMEM((4, 8, rows), f32),
+            pltpu.VMEM((4, 8, rows), f32),
+            pltpu.SemaphoreType.DMA((22,)),
+            pltpu.SemaphoreType.DMA((22,)),
+        ],
+        compiler_params=pltpu.CompilerParams(
+            collective_id=0, has_side_effects=True, vmem_limit_bytes=48 * 1024 * 1024
+        ),
+    )(
+        image_embed,
+        report_embed,
+        id_rows(image_study),
+        id_rows(report_study_index),
+        logit_scale,
+        logit_bias,
+    )
+    return (loss[0, :1], image_grad, report_grad)
+
+
 def solution(mesh):
     return jax.shard_map(
-        body,
+        kernel_body if mesh.shape["blk"] == 16 else body,
         mesh=mesh,
         in_specs=(
             P(("groups", "blk"), None),

time: 142 us -> 78.5 us (0.55)
  Pallas kernels: 0 us -> 71.6 us
  blocking collectives: 57 us -> 0 us
  waiting for transfers between devices: 37.3 us -> 0 us
  starting transfers between devices: 22.1 us -> 0 us
  other arithmetic: 12.3 us -> 0 us
  matrix products: 7.47 us -> 0 us
  local copies, waits for them, and re-layouts: 0.67 us -> 4.71 us
  between operations: 4.57 us -> 1.98 us
    pallas_call x0 -> x1, Pallas kernels: none -> 71.6 us  [kernel_body(): pl.pallas_call(tile_kernel, out_shape=(jax.ShapeDtypeStruct((8, 128), f32...]
    psum x1 -> x0, blocking collectives: 57 us -> none  [body(): total = lax.psum(loss_part, 'blk')]
    ppermute x12 -> x0, waiting for transfers between devices: 37.3 us -> none  [from_partner(): lax.ppermute(value, axis, [(i, i ^ 1 << stride) for i in range(lax.axis_s...]
    ppermute x12 -> x0, starting transfers between devices: 22.1 us -> none  [from_partner(): lax.ppermute(value, axis, [(i, i ^ 1 << stride) for i in range(lax.axis_s...]
    dot_general x3 -> x0, matrix products: 7.47 us -> none  [the longest x1 3.75 us: step(): lax.dot_general(block_slice, reports, (((1,), (1,)), ((), ())), preferred...]
    add x2 -> x0, other arithmetic: 3.59 us -> none  [the longest x1 2.15 us: body(): image_part = keep + from_partner(give, 'blk', bit)]
    unnamed x14 -> x10, local copies, waits for them, and re-layouts: 0.67 us -> 4.19 us
    reduce_sum x4 -> x0, other arithmetic: 2.83 us -> none  [the longest x2 2.25 us: unit_rows(): norm = jnp.sqrt(jnp.sum(values * values, axis=1, keepdims=True) + 1e-06)]
  transfers between devices with their start and end apart: 12 -> 0, of which waited for: 4 -> 0; matrix products, arithmetic and copies ran while one was open for 6% -> 0% of each run, Pallas kernels for 0% -> 0%
where the time goes in v1:
time: 78.5 us; the launch traced here: 78.3 us
  Pallas kernels  71.6 us (91%)
  local copies, waits for them, and re-layouts  4.71 us (6%)
  between operations  1.98 us (3%)
    pallas_call x1, Pallas kernels, kernel_body(): pl.pallas_call(tile_kernel, out_shape=(jax.ShapeDtypeStruct((8, 128), f32...  71.6 us
    unnamed x10, local copies, waits for them, and re-layouts  4.19 us

profile of v1, /device:TPU:0, one launch (start us, length us, event | category | flops | bytes accessed | tf_op | source)
XLA Modules:
  0.0 78.3 jit_solution(7094452236840503639)
XLA Ops:
  1.3 0.0 copy-start.2
  1.9 0.0 copy-done.2
  2.0 0.0 copy-start.3
  2.0 0.6 copy-done.3
  2.6 0.0 copy-start
  2.6 1.0 %copy-done = bf16[128,1152]{1,0:T(8,128)(2,1)S(1)} copy-done((bf16[128,1152]{1,0:T(8,128)(2,1)S(1)}, bf16[128,1152]{1,0:T(8,128)(2,1)}, u32[]{:S(2)}) %copy-start) | copy-done | bytes 294936
  3.6 0.0 copy-start.1
  3.6 1.0 %copy-done.1 = bf16[128,1152]{1,0:T(8,128)(2,1)S(1)} copy-done((bf16[128,1152]{1,0:T(8,128)(2,1)S(1)}, bf16[128,1152]{1,0:T(8,128)(2,1)}, u32[]{:S(2)}) %copy-start.1) | copy-done | bytes 294936
  4.5 71.6 %shard_map.85 = (f32[8,128]{1,0:T(8,128)S(1)}, f32[128,1152]{1,0:T(8,128)S(1)}, f32[128,1152]{1,0:T(8,128)S(1)}) custom-call(bf16[128,1152]{1,0:T(8,128)(2,1)S(1)} %copy-done, bf16[128,1152]{1,0:T(8,128)(2,1)S(1)} %copy-done.1, s32[8,128]{1,0:T(8,128)S(1)} %broadcast_in_dim.4.image_id_ref, s32[8,128]{1,0:T(8,128)S(1)} %broadcast_in_dim.5.report_id_ref, ...), custom_call_target="tpu_custom_call" | custom-call | tf_op jit(solution)/shard_map/pallas_call | solution.py:300
  76.2 0.5 slice.3
  76.7 0.8 %copy.13 = f32[128,1152]{1,0:T(8,128)} copy(f32[128,1152]{1,0:T(8,128)S(1)} %get-tuple-element.13) | data formatting | bytes 1179648
  77.5 0.8 %copy.14 = f32[128,1152]{1,0:T(8,128)} copy(f32[128,1152]{1,0:T(8,128)S(1)} %get-tuple-element.14) | data formatting | bytes 1179648
  (2 shorter events, 0.0 us)
Async XLA Ops:
  1.3 0.7 copy-start.2
  2.0 0.7 copy-start.3
  2.6 1.0 %copy-start = (bf16[128,1152]{1,0:T(8,128)(2,1)S(1)}, bf16[128,1152]{1,0:T(8,128)(2,1)}, u32[]{:S(2)}) copy-start(bf16[128,1152]{1,0:T(8,128)(2,1)} %image_ref.1) | copy-start | bytes 884740
  3.6 1.0 %copy-start.1 = (bf16[128,1152]{1,0:T(8,128)(2,1)S(1)}, bf16[128,1152]{1,0:T(8,128)(2,1)}, u32[]{:S(2)}) copy-start(bf16[128,1152]{1,0:T(8,128)(2,1)} %report_ref.1) | copy-start | bytes 884740

commit v2 on v1

--- a/solution.py
+++ b/solution.py
@@ -117,19 +117,36 @@
 
 
 CORE, ACROSS, NEAR, FAR = (1, 2, 4, 8)
+PIECES = 4
+TOP = 32767.0
 MESH_ID = pl.DeviceIdType.MESH
 
 
+def encode(value, code_ref, step_ref):
+    peak = jnp.maximum(jnp.max(jnp.abs(value), axis=1, keepdims=True), 1e-30)
+    code_ref[...] = jnp.round(value * (TOP / peak)).astype(jnp.int32).astype(jnp.int16)
+    rows = value.shape[0]
+    step_ref[...] = jnp.broadcast_to(peak * (1.0 / TOP), (rows, rows)).T[:8]
+
+
+def decode(code_ref, step_ref):
+    code = code_ref[...].astype(jnp.int32).astype(jnp.float32)
+    rows = code.shape[0]
+    return code * jnp.broadcast_to(step_ref[0:1, :], (rows, rows)).T[:, :1]
+
+
 def tile_kernel(
-    image_ref, report_ref, image_id_ref, report_id_ref, scale_ref, bias_ref,
+    image_hbm, report_hbm, image_id_ref, report_id_ref, scale_ref, bias_ref,
     loss_ref, image_grad_ref, report_grad_ref,
-    images, reports, image_ids, report_ids, coeffs, image_part, report_part,
-    core_in, far_in, across_in, near_in, far_out, near_out, loss_out, loss_in,
-    send_sem, recv_sem,
+    image_ref, report_ref,
+    images, reports, image_ids, report_ids, coeffs, image_part, core_in,
+    codes_out, codes_in, steps_out, steps_in, loss_out, loss_in,
+    load_sem, send_sem, recv_sem,
 ):
     group = lax.axis_index("groups")
     me = lax.axis_index("blk")
     rows = image_ref.shape[0]
+    piece = rows // PIECES
 
     def partner(bit):
         low = lax.rem(lax.div(me, bit), 2)
@@ -147,6 +164,10 @@
         copy.start()
         return copy
 
+    report_load = pltpu.make_async_copy(report_hbm, report_ref, load_sem.at[0])
+    report_load.start()
+    image_load = pltpu.make_async_copy(image_hbm, image_ref, load_sem.at[1])
+    image_load.start()
     barrier = pltpu.get_barrier_semaphore()
     for bit in (CORE, ACROSS, NEAR, FAR):
         pl.semaphore_signal(barrier, inc=1, device_id=partner(bit), device_id_type=MESH_ID)
@@ -156,13 +177,20 @@
         norm = jnp.sqrt(jnp.sum(values * values, axis=1, keepdims=True) + 1e-06)
         return (norm, values / norm)
 
+    report_load.wait()
     reports[0] = normalised(report_ref)[1].astype(jnp.bfloat16)
+    image_load.wait()
     images[0] = normalised(image_ref)[1].astype(jnp.bfloat16)
-    image_ids[0] = image_id_ref[...]
-    report_ids[0] = report_id_ref[...]
+    image_ids[0] = jnp.broadcast_to(image_id_ref[...], (8, rows))
+    report_ids[0] = jnp.broadcast_to(report_id_ref[...], (8, rows))
     pl.semaphore_wait(barrier, 4)
 
-    report_near = send(0, reports.at[0], reports.at[2], NEAR)
+    def part(k):
+        return pl.ds(k * piece, piece)
+
+    report_near = [
+        send(32 + k, reports.at[0, part(k)], reports.at[2, part(k)], NEAR) for k in range(PIECES)
+    ]
     report_near_id = send(1, report_ids.at[0], report_ids.at[2], NEAR)
     report_across = send(2, reports.at[0], reports.at[1], ACROSS)
     report_across_id = send(3, report_ids.at[0], report_ids.at[1], ACROSS)
@@ -194,10 +222,14 @@
     image_core.wait()
     image_core_id.wait()
     total = tile(0, 0) + tile(1, 0)
-    report_near.wait()
     report_near_id.wait()
-    report_diag = send(8, reports.at[2], reports.at[3], ACROSS)
     report_diag_id = send(9, report_ids.at[2], report_ids.at[3], ACROSS)
+    report_diag = []
+    for k in range(PIECES):
+        report_near[k].wait()
+        report_diag.append(
+            send(32 + PIECES + k, reports.at[2, part(k)], reports.at[3, part(k)], ACROSS)
+        )
     total += tile(0, 2) + tile(1, 2)
     report_across.wait()
     report_across_id.wait()
@@ -210,7 +242,8 @@
     image_diag.wait()
     image_diag_id.wait()
     total += tile(3, 0) + tile(3, 1) + tile(3, 2)
-    report_diag.wait()
+    for copy in report_diag:
+        copy.wait()
     report_diag_id.wait()
     for i in range(4):
         total += tile(i, 3)
@@ -236,24 +269,35 @@
             out = term if out is None else out + term
         return scale * out
 
-    report_part[0] = report_sum(3)
-    across_first = send(12, report_part.at[0], across_in.at[0], ACROSS)
+    def send_coded(number, value, bit):
+        encode(value, codes_out.at[number], steps_out.at[number])
+        return (
+            send(12 + 2 * number, steps_out.at[number], steps_in.at[number], bit),
+            send(13 + 2 * number, codes_out.at[number], codes_in.at[number], bit),
+        )
+
+    def receive(copies, number):
+        for copy in copies:
+            copy.wait()
+        return decode(codes_in.at[number], steps_in.at[number])
+
+    across_first = send_coded(0, report_sum(3), ACROSS)
     image_part[0] = image_sum(3)
-    core_first = send(13, image_part.at[0], core_in.at[0], CORE)
+    core_first = send(20, image_part.at[0], core_in.at[0], CORE)
     far_sum = image_sum(2)
-    core_first.wait_recv()
-    far_out[...] = far_sum + core_in[0]
-    far_send = send(14, far_out, far_in, FAR)
-    report_part[1] = report_sum(1)
-    across_second = send(15, report_part.at[1], across_in.at[1], ACROSS)
+    core_first.wait()
+    far = send_coded(1, far_sum + core_in[0], FAR)
+    across_sum = report_sum(1)
+    near_sum = report_sum(2)
+    near = send_coded(2, near_sum + receive(across_first, 0), NEAR)
+    across_second = send_coded(3, across_sum, ACROSS)
     image_part[1] = image_sum(1)
-    core_second = send(16, image_part.at[1], core_in.at[1], CORE)
-    near_sum = report_sum(2)
+    core_second = send(21, image_part.at[1], core_in.at[1], CORE)
 
     loss_out[0] = jnp.sum(total.reshape(rows // 8, 8, rows), axis=0)
     loss_copies = []
     for step, bit in enumerate((CORE, ACROSS, NEAR, FAR)):
-        copy = send(18 + step, loss_out.at[step], loss_in.at[step], bit)
+        copy = send(22 + step, loss_out.at[step], loss_in.at[step], bit)
         if step == 0:
             own_image = image_sum(0)
         elif step == 1:
@@ -266,36 +310,23 @@
     pairs = rows * lax.axis_size("blk")
     loss_ref[...] = jnp.full(loss_ref.shape, jnp.sum(whole) / pairs, jnp.float32)
 
-    across_first.wait_recv()
-    near_out[...] = near_sum + across_in[0]
-    near_send = send(17, near_out, near_in, NEAR)
-
     def finish(ref, unit_grad):
         norm, unit = normalised(ref)
         return (unit_grad - unit * jnp.sum(unit * unit_grad, axis=1, keepdims=True)) / norm
 
-    core_second.wait_recv()
+    core_second.wait()
     own_image += core_in[1]
-    far_send.wait()
-    image_grad_ref[...] = finish(image_ref, own_image + far_in[...])
-    across_second.wait_recv()
-    own_report += across_in[1]
-    near_send.wait()
-    report_grad_ref[...] = finish(report_ref, own_report + near_in[...])
-    across_first.wait_send()
-    across_second.wait_send()
-    core_first.wait_send()
-    core_second.wait_send()
+    image_grad_ref[...] = finish(image_ref, own_image + receive(far, 1))
+    own_report += receive(across_second, 3)
+    report_grad_ref[...] = finish(report_ref, own_report + receive(near, 2))
 
 
 def kernel_body(image_embed, report_embed, image_study, report_study_index, logit_scale, logit_bias):
     rows, width = image_embed.shape
     f32 = jnp.float32
 
-    def id_rows(ids):
-        return jnp.broadcast_to(ids[None, :], (8, rows))
-
     vmem = pl.BlockSpec(memory_space=pltpu.VMEM)
+    hbm = pl.BlockSpec(memory_space=pl.ANY)
     smem = pl.BlockSpec(memory_space=pltpu.SMEM)
     loss, image_grad, report_grad = pl.pallas_call(
         tile_kernel,
@@ -304,9 +335,11 @@
             jax.ShapeDtypeStruct((rows, width), f32),
             jax.ShapeDtypeStruct((rows, width), f32),
         ),
-        in_specs=[vmem, vmem, vmem, vmem, smem, smem],
+        in_specs=[hbm, hbm, vmem, vmem, smem, smem],
         out_specs=(vmem, vmem, vmem),
         scratch_shapes=[
+            pltpu.VMEM((rows, width), jnp.bfloat16),
+            pltpu.VMEM((rows, width), jnp.bfloat16),
             pltpu.VMEM((4, rows, width), jnp.bfloat16),
             pltpu.VMEM((4, rows, width), jnp.bfloat16),
             pltpu.VMEM((4, 8, rows), jnp.int32),
@@ -314,16 +347,15 @@
             pltpu.VMEM((4, rows, 4 * rows), jnp.bfloat16),
             pltpu.VMEM((2, rows, width), f32),
             pltpu.VMEM((2, rows, width), f32),
-            pltpu.VMEM((2, rows, width), f32),
-            pltpu.VMEM((rows, width), f32),
-            pltpu.VMEM((2, rows, width), f32),
-            pltpu.VMEM((rows, width), f32),
-            pltpu.VMEM((rows, width), f32),
-            pltpu.VMEM((rows, width), f32),
+            pltpu.VMEM((4, rows, width), jnp.int16),
+            pltpu.VMEM((4, rows, width), jnp.int16),
             pltpu.VMEM((4, 8, rows), f32),
             pltpu.VMEM((4, 8, rows), f32),
-            pltpu.SemaphoreType.DMA((22,)),
-            pltpu.SemaphoreType.DMA((22,)),
+            pltpu.VMEM((4, 8, rows), f32),
+            pltpu.VMEM((4, 8, rows), f32),
+            pltpu.SemaphoreType.DMA((2,)),
+            pltpu.SemaphoreType.DMA((32 + 2 * PIECES,)),
+            pltpu.SemaphoreType.DMA((32 + 2 * PIECES,)),
         ],
         compiler_params=pltpu.CompilerParams(
             collective_id=0, has_side_effects=True, vmem_limit_bytes=48 * 1024 * 1024
@@ -331,8 +363,8 @@
     )(
         image_embed,
         report_embed,
-        id_rows(image_study),
-        id_rows(report_study_index),
+        image_study.reshape(1, rows),
+        report_study_index.reshape(1, rows),
         logit_scale,
         logit_bias,
     )

time: 78.5 us -> 56.9 us (0.72)
  Pallas kernels: 71.6 us -> 50 us
    pallas_call x1, Pallas kernels: 71.6 us -> 50 us  [kernel_body(): pl.pallas_call(tile_kernel, out_shape=(jax.ShapeDtypeStruct((8, 128), f32...]
where the time goes in v2:
time: 56.9 us; the launch traced here: 56.6 us
  Pallas kernels  50 us (88%)
  local copies, waits for them, and re-layouts  4.72 us (8%)
  between operations  1.95 us (3%)
    pallas_call x1, Pallas kernels, kernel_body(): pl.pallas_call(tile_kernel, out_shape=(jax.ShapeDtypeStruct((8, 128), f32...  50 us
    unnamed x10, local copies, waits for them, and re-layouts  4.21 us

profile of v2, /device:TPU:0, one launch (start us, length us, event | category | flops | bytes accessed | tf_op | source)
XLA Modules:
  0.0 56.6 jit_solution(17152112324045287360)
XLA Ops:
  1.9 0.0 copy-start.2
  1.9 0.0 copy-start.3
  1.9 0.6 %copy-done.2 = s32[128]{0:T(128)S(1)} copy-done((s32[128]{0:T(128)S(1)}, s32[128]{0:T(128)}, u32[]{:S(2)}) %copy-start.2) | copy-done | bytes 536
  2.6 0.0 copy-done.3
  2.6 0.0 copy-start
  2.6 1.0 %copy-done = bf16[128,1152]{1,0:T(8,128)(2,1)S(1)} copy-done((bf16[128,1152]{1,0:T(8,128)(2,1)S(1)}, bf16[128,1152]{1,0:T(8,128)(2,1)}, u32[]{:S(2)}) %copy-start) | copy-done | bytes 294936
  3.6 0.0 copy-start.1
  3.6 1.0 %copy-done.1 = bf16[128,1152]{1,0:T(8,128)(2,1)S(1)} copy-done((bf16[128,1152]{1,0:T(8,128)(2,1)S(1)}, bf16[128,1152]{1,0:T(8,128)(2,1)}, u32[]{:S(2)}) %copy-start.1) | copy-done | bytes 294936
  4.5 50.0 %shard_map.85 = (f32[8,128]{1,0:T(8,128)S(1)}, f32[128,1152]{1,0:T(8,128)S(1)}, f32[128,1152]{1,0:T(8,128)S(1)}) custom-call(bf16[128,1152]{1,0:T(8,128)(2,1)S(1)} %copy-done, bf16[128,1152]{1,0:T(8,128)(2,1)S(1)} %copy-done.1, s32[1,128]{1,0:T(1,128)S(1)} %bitcast.3, s32[1,128]{1,0:T(1,128)S(1)} %bitcast.4, f32[1]{0:T(128)S(6)} %copy.11.scale_ref, ...), custom_call_target="tpu_custom_call" | custom-call | tf_op jit(solution)/shard_map/pallas_call | solution.py:331
  54.5 0.5 slice.3
  55.0 0.8 %copy.13 = f32[128,1152]{1,0:T(8,128)} copy(f32[128,1152]{1,0:T(8,128)S(1)} %get-tuple-element.13) | data formatting | bytes 1179648
  55.8 0.8 %copy.14 = f32[128,1152]{1,0:T(8,128)} copy(f32[128,1152]{1,0:T(8,128)S(1)} %get-tuple-element.14) | data formatting | bytes 1179648
Async XLA Ops:
  1.9 0.7 %copy-start.2 = (s32[128]{0:T(128)S(1)}, s32[128]{0:T(128)}, u32[]{:S(2)}) copy-start(s32[128]{0:T(128)} %param.8) | copy-start | bytes 1540
  1.9 0.7 %copy-start.3 = (s32[128]{0:T(128)S(1)}, s32[128]{0:T(128)}, u32[]{:S(2)}) copy-start(s32[128]{0:T(128)} %param.9) | copy-start | bytes 1540
  2.6 1.0 %copy-start = (bf16[128,1152]{1,0:T(8,128)(2,1)S(1)}, bf16[128,1152]{1,0:T(8,128)(2,1)}, u32[]{:S(2)}) copy-start(bf16[128,1152]{1,0:T(8,128)(2,1)} %image_hbm.1) | copy-start | bytes 884740
  3.6 1.0 %copy-start.1 = (bf16[128,1152]{1,0:T(8,128)(2,1)S(1)}, bf16[128,1152]{1,0:T(8,128)(2,1)}, u32[]{:S(2)}) copy-start(bf16[128,1152]{1,0:T(8,128)(2,1)} %report_hbm.1) | copy-start | bytes 884740

commit v3 on v2

--- a/solution.py
+++ b/solution.py
@@ -122,24 +122,29 @@
 MESH_ID = pl.DeviceIdType.MESH
 
 
+def turned(column, rows):
+    square = jnp.broadcast_to(column, (column.shape[0], rows))
+    return jnp.concatenate([square] * (rows // column.shape[0]), axis=0).T
+
+
 def encode(value, code_ref, step_ref):
     peak = jnp.maximum(jnp.max(jnp.abs(value), axis=1, keepdims=True), 1e-30)
     code_ref[...] = jnp.round(value * (TOP / peak)).astype(jnp.int32).astype(jnp.int16)
-    rows = value.shape[0]
-    step_ref[...] = jnp.broadcast_to(peak * (1.0 / TOP), (rows, rows)).T[:8]
+    step_ref[...] = turned(peak * (1.0 / TOP), step_ref.shape[1])[:8]
 
 
 def decode(code_ref, step_ref):
     code = code_ref[...].astype(jnp.int32).astype(jnp.float32)
-    rows = code.shape[0]
-    return code * jnp.broadcast_to(step_ref[0:1, :], (rows, rows)).T[:, :1]
+    rows = step_ref.shape[1]
+    step = jnp.broadcast_to(step_ref[0:1, :], (rows, rows)).T[: code.shape[0], :1]
+    return code * step
 
 
 def tile_kernel(
-    image_hbm, report_hbm, image_id_ref, report_id_ref, scale_ref, bias_ref,
+    image_hbm, report_hbm, image_id_hbm, report_id_hbm, scale_ref, bias_ref,
     loss_ref, image_grad_ref, report_grad_ref,
-    image_ref, report_ref,
-    images, reports, image_ids, report_ids, coeffs, image_part, core_in,
+    image_ref, report_ref, image_id_ref, report_id_ref,
+    images, reports, image_ids, report_ids, coeffs, image_part, report_part, core_in,
     codes_out, codes_in, steps_out, steps_in, loss_out, loss_in,
     load_sem, send_sem, recv_sem,
 ):
@@ -164,10 +169,15 @@
         copy.start()
         return copy
 
-    report_load = pltpu.make_async_copy(report_hbm, report_ref, load_sem.at[0])
-    report_load.start()
-    image_load = pltpu.make_async_copy(image_hbm, image_ref, load_sem.at[1])
-    image_load.start()
+    loads = []
+    for source, target in (
+        (report_hbm, report_ref),
+        (image_hbm, image_ref),
+        (report_id_hbm, report_id_ref),
+        (image_id_hbm, image_id_ref),
+    ):
+        loads.append(pltpu.make_async_copy(source, target, load_sem.at[len(loads)]))
+        loads[-1].start()
     barrier = pltpu.get_barrier_semaphore()
     for bit in (CORE, ACROSS, NEAR, FAR):
         pl.semaphore_signal(barrier, inc=1, device_id=partner(bit), device_id_type=MESH_ID)
@@ -177,10 +187,12 @@
         norm = jnp.sqrt(jnp.sum(values * values, axis=1, keepdims=True) + 1e-06)
         return (norm, values / norm)
 
-    report_load.wait()
+    loads[0].wait()
     reports[0] = normalised(report_ref)[1].astype(jnp.bfloat16)
-    image_load.wait()
+    loads[1].wait()
     images[0] = normalised(image_ref)[1].astype(jnp.bfloat16)
+    loads[2].wait()
+    loads[3].wait()
     image_ids[0] = jnp.broadcast_to(image_id_ref[...], (8, rows))
     report_ids[0] = jnp.broadcast_to(report_id_ref[...], (8, rows))
     pl.semaphore_wait(barrier, 4)
@@ -188,9 +200,10 @@
     def part(k):
         return pl.ds(k * piece, piece)
 
-    report_near = [
-        send(32 + k, reports.at[0, part(k)], reports.at[2, part(k)], NEAR) for k in range(PIECES)
-    ]
+    def near_piece(k):
+        return send(32 + k, reports.at[0, part(k)], reports.at[2, part(k)], NEAR)
+
+    report_near = [near_piece(0), near_piece(1)]
     report_near_id = send(1, report_ids.at[0], report_ids.at[2], NEAR)
     report_across = send(2, reports.at[0], reports.at[1], ACROSS)
     report_across_id = send(3, report_ids.at[0], report_ids.at[1], ACROSS)
@@ -227,6 +240,8 @@
     report_diag = []
     for k in range(PIECES):
         report_near[k].wait()
+        if k + 2 < PIECES:
+            report_near.append(near_piece(k + 2))
         report_diag.append(
             send(32 + PIECES + k, reports.at[2, part(k)], reports.at[3, part(k)], ACROSS)
         )
@@ -242,21 +257,6 @@
     image_diag.wait()
     image_diag_id.wait()
     total += tile(3, 0) + tile(3, 1) + tile(3, 2)
-    for copy in report_diag:
-        copy.wait()
-    report_diag_id.wait()
-    for i in range(4):
-        total += tile(i, 3)
-
-    def image_sum(i):
-        out = None
-        for j in range(4):
-            term = jnp.dot(
-                coeffs[i, :, j * rows : (j + 1) * rows], reports[j], preferred_element_type=jnp.float32
-            )
-            out = term if out is None else out + term
-        return scale * out
-
     def report_sum(j):
         out = None
         for i in range(4):
@@ -269,28 +269,60 @@
             out = term if out is None else out + term
         return scale * out
 
+    report_part[0] = report_sum(1)
+    report_part[1] = report_sum(2)
+    early = reports[:3].reshape(3 * rows, images.shape[2])
+    for i in (3, 2, 1, 0):
+        image_part[i] = scale * jnp.dot(
+            coeffs[i, :, : 3 * rows], early, preferred_element_type=jnp.float32
+        )
+
+    def image_sum(i):
+        return image_part[i] + scale * jnp.dot(
+            coeffs[i, :, 3 * rows :], reports[3], preferred_element_type=jnp.float32
+        )
+
+    for copy in report_diag:
+        copy.wait()
+    report_diag_id.wait()
+    for i in range(4):
+        total += tile(i, 3)
+
     def send_coded(number, value, bit):
-        encode(value, codes_out.at[number], steps_out.at[number])
-        return (
-            send(12 + 2 * number, steps_out.at[number], steps_in.at[number], bit),
-            send(13 + 2 * number, codes_out.at[number], codes_in.at[number], bit),
-        )
-
-    def receive(copies, number):
+        slot, first = divmod(number, PIECES)
+        height = value.shape[0]
+        lines = pl.ds(first * height, height)
+        encode(value, codes_out.at[slot, lines], steps_out.at[number])
+        return [
+            send(40 + 2 * number, steps_out.at[number], steps_in.at[number], bit),
+            send(
+                41 + 2 * number, codes_out.at[slot, lines], codes_in.at[slot, lines], bit
+            ),
+        ]
+
+    def receive(copies, number, height):
+        slot, first = divmod(number, PIECES)
         for copy in copies:
             copy.wait()
-        return decode(codes_in.at[number], steps_in.at[number])
-
-    across_first = send_coded(0, report_sum(3), ACROSS)
-    image_part[0] = image_sum(3)
-    core_first = send(20, image_part.at[0], core_in.at[0], CORE)
-    far_sum = image_sum(2)
+        return decode(codes_in.at[slot, pl.ds(first * height, height)], steps_in.at[number])
+
+    reports_sum = report_sum(3)
+    pieces = [reports_sum[k * piece : (k + 1) * piece] for k in range(PIECES)]
+    across_first = [send_coded(k, pieces[k], ACROSS) for k in range(2)]
+    image_part[3] = image_sum(3)
+    core_first = send(20, image_part.at[3], core_in.at[0], CORE)
+    for k in range(2, PIECES):
+        report_part[2, part(k)] = pieces[k]
+    image_part[2] = image_sum(2)
     core_first.wait()
-    far = send_coded(1, far_sum + core_in[0], FAR)
-    across_sum = report_sum(1)
-    near_sum = report_sum(2)
-    near = send_coded(2, near_sum + receive(across_first, 0), NEAR)
-    across_second = send_coded(3, across_sum, ACROSS)
+    far = send_coded(3 * PIECES, image_part[2] + core_in[0], FAR)
+    near = []
+    for k in range(PIECES):
+        landed = receive(across_first[k], k, piece)
+        near.append(send_coded(PIECES + k, report_part[1, part(k)] + landed, NEAR))
+        if k + 2 < PIECES:
+            across_first.append(send_coded(k + 2, report_part[2, part(k + 2)], ACROSS))
+    across_second = send_coded(2 * PIECES, report_part[0], ACROSS)
     image_part[1] = image_sum(1)
     core_second = send(21, image_part.at[1], core_in.at[1], CORE)
 
@@ -316,9 +348,11 @@
 
     core_second.wait()
     own_image += core_in[1]
-    image_grad_ref[...] = finish(image_ref, own_image + receive(far, 1))
-    own_report += receive(across_second, 3)
-    report_grad_ref[...] = finish(report_ref, own_report + receive(near, 2))
+    image_grad_ref[...] = finish(image_ref, own_image + receive(far, 3 * PIECES, rows))
+    own_report += receive(across_second, 2 * PIECES, rows)
+    for k in range(PIECES):
+        report_part[0, part(k)] = receive(near[k], PIECES + k, piece)
+    report_grad_ref[...] = finish(report_ref, own_report + report_part[0])
 
 
 def kernel_body(image_embed, report_embed, image_study, report_study_index, logit_scale, logit_bias):
@@ -335,30 +369,33 @@
             jax.ShapeDtypeStruct((rows, width), f32),
             jax.ShapeDtypeStruct((rows, width), f32),
         ),
-        in_specs=[hbm, hbm, vmem, vmem, smem, smem],
+        in_specs=[hbm, hbm, hbm, hbm, smem, smem],
         out_specs=(vmem, vmem, vmem),
         scratch_shapes=[
             pltpu.VMEM((rows, width), jnp.bfloat16),
             pltpu.VMEM((rows, width), jnp.bfloat16),
+            pltpu.VMEM((1, rows), jnp.int32),
+            pltpu.VMEM((1, rows), jnp.int32),
             pltpu.VMEM((4, rows, width), jnp.bfloat16),
             pltpu.VMEM((4, rows, width), jnp.bfloat16),
             pltpu.VMEM((4, 8, rows), jnp.int32),
             pltpu.VMEM((4, 8, rows), jnp.int32),
             pltpu.VMEM((4, rows, 4 * rows), jnp.bfloat16),
-            pltpu.VMEM((2, rows, width), f32),
+            pltpu.VMEM((4, rows, width), f32),
+            pltpu.VMEM((3, rows, width), f32),
             pltpu.VMEM((2, rows, width), f32),
             pltpu.VMEM((4, rows, width), jnp.int16),
             pltpu.VMEM((4, rows, width), jnp.int16),
+            pltpu.VMEM((4 * PIECES, 8, rows), f32),
+            pltpu.VMEM((4 * PIECES, 8, rows), f32),
             pltpu.VMEM((4, 8, rows), f32),
             pltpu.VMEM((4, 8, rows), f32),
-            pltpu.VMEM((4, 8, rows), f32),
-            pltpu.VMEM((4, 8, rows), f32),
-            pltpu.SemaphoreType.DMA((2,)),
-            pltpu.SemaphoreType.DMA((32 + 2 * PIECES,)),
-            pltpu.SemaphoreType.DMA((32 + 2 * PIECES,)),
+            pltpu.SemaphoreType.DMA((4,)),
+            pltpu.SemaphoreType.DMA((40 + 8 * PIECES,)),
+            pltpu.SemaphoreType.DMA((40 + 8 * PIECES,)),
         ],
         compiler_params=pltpu.CompilerParams(
-            collective_id=0, has_side_effects=True, vmem_limit_bytes=48 * 1024 * 1024
+            collective_id=0, has_side_effects=True, vmem_limit_bytes=60 * 1024 * 1024
         ),
     )(
         image_embed,

time: 56.9 us -> 57.2 us (level)
  Pallas kernels: 50 us -> 51.1 us
  local copies, waits for them, and re-layouts: 4.72 us -> 3.98 us
    unnamed x10 -> x4, local copies, waits for them, and re-layouts: 4.21 us -> 2.8 us
    pallas_call x1, Pallas kernels: 50 us -> 51.1 us  [kernel_body(): pl.pallas_call(tile_kernel, out_shape=(jax.ShapeDtypeStruct((8, 128), f32...]
    slice x1, local copies, waits for them, and re-layouts: 0.51 us -> 1.18 us  [kernel_body(): return (loss[0, :1], image_grad, report_grad)]
where the time goes in v3:
time: 57.2 us; the launch traced here: 57 us
  Pallas kernels  51.1 us (89%)
  local copies, waits for them, and re-layouts  3.98 us (7%)
  between operations  1.93 us (3%)
    pallas_call x1, Pallas kernels, kernel_body(): pl.pallas_call(tile_kernel, out_shape=(jax.ShapeDtypeStruct((8, 128), f32...  51.1 us
    unnamed x4, local copies, waits for them, and re-layouts  2.8 us
    slice x1, local copies, waits for them, and re-layouts, kernel_body(): return (loss[0, :1], image_grad, report_grad)  1.18 us

profile of v3, /device:TPU:0, one launch (start us, length us, event | category | flops | bytes accessed | tf_op | source)
XLA Modules:
  0.0 57.0 jit_solution(14374307684586226416)
XLA Ops:
  1.9 51.1 %shard_map.85 = (f32[8,128]{1,0:T(8,128)}, f32[128,1152]{1,0:T(8,128)}, f32[128,1152]{1,0:T(8,128)}) custom-call(bf16[128,1152]{1,0:T(8,128)(2,1)} %image_hbm.1, bf16[128,1152]{1,0:T(8,128)(2,1)} %report_hbm.1, s32[1,128]{1,0:T(1,128)} %bitcast.3, s32[1,128]{1,0:T(1,128)} %bitcast.4, f32[1]{0:T(128)S(6)} %copy.11.scale_ref, f32[1]{0:T(128)S(6)} %copy.12.bias_ref), custom_call_target="tpu_custom_call" | custom-call | tf_op jit(solution)/shard_map/pallas_call | solution.py:365
  53.0 1.2 %slice.3 = f32[1,1]{1,0:T(1,128)} slice(f32[8,128]{1,0:T(8,128)} %get-tuple-element.6), slice={[0:1], [0:1]} | slice | bytes 8 | tf_op jit(solution)/shard_map/slice | solution.py:408
  54.2 0.0 copy-start
  54.2 2.0 %copy.13 = f32[128,1152]{1,0:T(8,128)} copy(f32[128,1152]{1,0:T(8,128)} %get-tuple-element.13) | data formatting | bytes 1179648
  56.2 0.0 copy-done
  56.2 0.8 %copy.14 = f32[128,1152]{1,0:T(8,128)} copy(f32[128,1152]{1,0:T(8,128)S(1)} %copy-done) | data formatting | bytes 1179648
Async XLA Ops:
  54.2 2.0 %copy-start = (f32[128,1152]{1,0:T(8,128)S(1)}, f32[128,1152]{1,0:T(8,128)}, u32[]{:S(2)}) copy-start(f32[128,1152]{1,0:T(8,128)} %get-tuple-element.14) | copy-start | bytes 1769476

commit v4 on v3

--- a/solution.py
+++ b/solution.py
@@ -269,30 +269,9 @@
             out = term if out is None else out + term
         return scale * out
 
-    report_part[0] = report_sum(1)
-    report_part[1] = report_sum(2)
-    early = reports[:3].reshape(3 * rows, images.shape[2])
-    for i in (3, 2, 1, 0):
-        image_part[i] = scale * jnp.dot(
-            coeffs[i, :, : 3 * rows], early, preferred_element_type=jnp.float32
-        )
-
-    def image_sum(i):
-        return image_part[i] + scale * jnp.dot(
-            coeffs[i, :, 3 * rows :], reports[3], preferred_element_type=jnp.float32
-        )
-
-    for copy in report_diag:
-        copy.wait()
-    report_diag_id.wait()
-    for i in range(4):
-        total += tile(i, 3)
-
-    def send_coded(number, value, bit):
+    def coded(number, height, bit):
         slot, first = divmod(number, PIECES)
-        height = value.shape[0]
         lines = pl.ds(first * height, height)
-        encode(value, codes_out.at[slot, lines], steps_out.at[number])
         return [
             send(40 + 2 * number, steps_out.at[number], steps_in.at[number], bit),
             send(
@@ -300,47 +279,81 @@
             ),
         ]
 
+    def put(number, value):
+        slot, first = divmod(number, PIECES)
+        height = value.shape[0]
+        encode(value, codes_out.at[slot, pl.ds(first * height, height)], steps_out.at[number])
+
     def receive(copies, number, height):
         slot, first = divmod(number, PIECES)
         for copy in copies:
             copy.wait()
         return decode(codes_in.at[slot, pl.ds(first * height, height)], steps_in.at[number])
 
+    def loss_step(step):
+        return send(
+            22 + step, loss_out.at[step], loss_in.at[step], (CORE, ACROSS, NEAR, FAR)[step]
+        )
+
+    across_sum = report_sum(1)
+    for k in range(PIECES):
+        put(2 * PIECES + k, across_sum[k * piece : (k + 1) * piece])
+    report_part[1] = report_sum(2)
+    early = reports[:3].reshape(3 * rows, images.shape[2])
+    for i in (3, 2, 1, 0):
+        image_part[i] = scale * jnp.dot(
+            coeffs[i, :, : 3 * rows], early, preferred_element_type=jnp.float32
+        )
+
+    def image_sum(i):
+        return image_part[i] + scale * jnp.dot(
+            coeffs[i, :, 3 * rows :], reports[3], preferred_element_type=jnp.float32
+        )
+
+    for copy in report_diag:
+        copy.wait()
+    report_diag_id.wait()
+    across_second = [coded(2 * PIECES + k, piece, ACROSS) for k in range(2)]
+    for i in range(4):
+        total += tile(i, 3)
+    loss_out[0] = jnp.sum(total.reshape(rows // 8, 8, rows), axis=0)
+    loss_copy = loss_step(0)
     reports_sum = report_sum(3)
-    pieces = [reports_sum[k * piece : (k + 1) * piece] for k in range(PIECES)]
-    across_first = [send_coded(k, pieces[k], ACROSS) for k in range(2)]
+    for k in range(PIECES):
+        put(k, reports_sum[k * piece : (k + 1) * piece])
+    across_first = [coded(k, piece, ACROSS) for k in range(2)]
     image_part[3] = image_sum(3)
     core_first = send(20, image_part.at[3], core_in.at[0], CORE)
-    for k in range(2, PIECES):
-        report_part[2, part(k)] = pieces[k]
     image_part[2] = image_sum(2)
+    loss_copy.wait()
+    loss_out[1] = loss_out[0] + loss_in[0]
+    loss_copy = loss_step(1)
     core_first.wait()
-    far = send_coded(3 * PIECES, image_part[2] + core_in[0], FAR)
+    put(3 * PIECES, image_part[2] + core_in[0])
+    far = coded(3 * PIECES, rows, FAR)
     near = []
     for k in range(PIECES):
         landed = receive(across_first[k], k, piece)
-        near.append(send_coded(PIECES + k, report_part[1, part(k)] + landed, NEAR))
+        put(PIECES + k, report_part[1, part(k)] + landed)
+        near.append(coded(PIECES + k, piece, NEAR))
         if k + 2 < PIECES:
-            across_first.append(send_coded(k + 2, report_part[2, part(k + 2)], ACROSS))
-    across_second = send_coded(2 * PIECES, report_part[0], ACROSS)
-    image_part[1] = image_sum(1)
-    core_second = send(21, image_part.at[1], core_in.at[1], CORE)
-
-    loss_out[0] = jnp.sum(total.reshape(rows // 8, 8, rows), axis=0)
-    loss_copies = []
-    for step, bit in enumerate((CORE, ACROSS, NEAR, FAR)):
-        copy = send(22 + step, loss_out.at[step], loss_in.at[step], bit)
-        if step == 0:
+            across_first.append(coded(k + 2, piece, ACROSS))
+        else:
+            across_second.append(coded(2 * PIECES + k, piece, ACROSS))
+        if k == 0:
+            image_part[1] = image_sum(1)
+            core_second = send(21, image_part.at[1], core_in.at[1], CORE)
+        elif k == 1:
+            loss_copy.wait()
+            loss_out[2] = loss_out[1] + loss_in[1]
+            loss_copy = loss_step(2)
+        elif k == 2:
             own_image = image_sum(0)
-        elif step == 1:
+        else:
             own_report = report_sum(0)
-        copy.wait()
-        if step < 3:
-            loss_out[step + 1] = loss_out[step] + loss_in[step]
-        else:
-            whole = loss_out[step] + loss_in[step]
-    pairs = rows * lax.axis_size("blk")
-    loss_ref[...] = jnp.full(loss_ref.shape, jnp.sum(whole) / pairs, jnp.float32)
+    loss_copy.wait()
+    loss_out[3] = loss_out[2] + loss_in[2]
+    loss_copy = loss_step(3)
 
     def finish(ref, unit_grad):
         norm, unit = normalised(ref)
@@ -349,10 +362,16 @@
     core_second.wait()
     own_image += core_in[1]
     image_grad_ref[...] = finish(image_ref, own_image + receive(far, 3 * PIECES, rows))
-    own_report += receive(across_second, 2 * PIECES, rows)
-    for k in range(PIECES):
-        report_part[0, part(k)] = receive(near[k], PIECES + k, piece)
-    report_grad_ref[...] = finish(report_ref, own_report + report_part[0])
+    loss_copy.wait()
+    pairs = rows * lax.axis_size("blk")
+    loss = jnp.sum(loss_out[3] + loss_in[3]) / pairs
+    loss_ref[...] = jnp.full(loss_ref.shape, loss, jnp.float32)
+    report_part[0] = own_report
+    for k in range(PIECES):
+        report_part[0, part(k)] += receive(across_second[k], 2 * PIECES + k, piece)
+    for k in range(PIECES):
+        report_part[0, part(k)] += receive(near[k], PIECES + k, piece)
+    report_grad_ref[...] = finish(report_ref, report_part[0])
 
 
 def kernel_body(image_embed, report_embed, image_study, report_study_index, logit_scale, logit_bias):
@@ -360,7 +379,7 @@
     f32 = jnp.float32
 
     vmem = pl.BlockSpec(memory_space=pltpu.VMEM)
-    hbm = pl.BlockSpec(memory_space=pl.ANY)
+    hbm = pl.BlockSpec(memory_space=pltpu.HBM)
     smem = pl.BlockSpec(memory_space=pltpu.SMEM)
     loss, image_grad, report_grad = pl.pallas_call(
         tile_kernel,
@@ -382,7 +401,7 @@
             pltpu.VMEM((4, 8, rows), jnp.int32),
             pltpu.VMEM((4, rows, 4 * rows), jnp.bfloat16),
             pltpu.VMEM((4, rows, width), f32),
-            pltpu.VMEM((3, rows, width), f32),
+            pltpu.VMEM((2, rows, width), f32),
             pltpu.VMEM((2, rows, width), f32),
             pltpu.VMEM((4, rows, width), jnp.int16),
             pltpu.VMEM((4, rows, width), jnp.int16),
@@ -395,13 +414,13 @@
             pltpu.SemaphoreType.DMA((40 + 8 * PIECES,)),
         ],
         compiler_params=pltpu.CompilerParams(
-            collective_id=0, has_side_effects=True, vmem_limit_bytes=60 * 1024 * 1024
+            collective_id=0, has_side_effects=True, vmem_limit_bytes=48 * 1024 * 1024
         ),
     )(
-        image_embed,
-        report_embed,
-        image_study.reshape(1, rows),
-        report_study_index.reshape(1, rows),
+        pltpu.with_memory_space_constraint(image_embed, pltpu.HBM),
+        pltpu.with_memory_space_constraint(report_embed, pltpu.HBM),
+        pltpu.with_memory_space_constraint(image_study.reshape(1, rows), pltpu.HBM),
+        pltpu.with_memory_space_constraint(report_study_index.reshape(1, rows), pltpu.HBM),
         logit_scale,
         logit_bias,
     )

time: 57.2 us -> 51.6 us (0.902)
  Pallas kernels: 51.1 us -> 47.3 us
  local copies, waits for them, and re-layouts: 3.98 us -> 2.14 us
    pallas_call x1, Pallas kernels: 51.1 us -> 47.3 us  [kernel_body(): pl.pallas_call(tile_kernel, out_shape=(jax.ShapeDtypeStruct((8, 128), f32...]
    unnamed x4 -> x2, local copies, waits for them, and re-layouts: 2.8 us -> 1.63 us
    slice x1, local copies, waits for them, and re-layouts: 1.18 us -> 0.51 us  [kernel_body(): return (loss[0, :1], image_grad, report_grad)]
where the time goes in v4:
time: 51.6 us; the launch traced here: 51.4 us
  Pallas kernels  47.3 us (92%)
  local copies, waits for them, and re-layouts  2.14 us (4%)
  between operations  1.93 us (4%)
    pallas_call x1, Pallas kernels, kernel_body(): pl.pallas_call(tile_kernel, out_shape=(jax.ShapeDtypeStruct((8, 128), f32...  47.3 us
    unnamed x2, local copies, waits for them, and re-layouts  1.63 us

profile of v4, /device:TPU:0, one launch (start us, length us, event | category | flops | bytes accessed | tf_op | source)
XLA Modules:
  0.0 51.4 jit_solution(4647899948343025537)
XLA Ops:
  1.9 47.3 %shard_map.85 = (f32[8,128]{1,0:T(8,128)S(1)}, f32[128,1152]{1,0:T(8,128)S(1)}, f32[128,1152]{1,0:T(8,128)S(1)}) custom-call(bf16[128,1152]{1,0:T(8,128)(2,1)} %image_hbm.1, bf16[128,1152]{1,0:T(8,128)(2,1)} %report_hbm.1, s32[1,128]{1,0:T(1,128)} %bitcast.3, s32[1,128]{1,0:T(1,128)} %bitcast.4, f32[1]{0:T(128)S(6)} %copy.11.scale_ref, f32[1]{0:T(128)S(6)} %copy.12.bias_ref), custom_call_target="tpu_custom_call" | custom-call | tf_op jit(solution)/shard_map/pallas_call | solution.py:384
  49.3 0.5 slice.3
  49.8 0.8 %copy.13 = f32[128,1152]{1,0:T(8,128)} copy(f32[128,1152]{1,0:T(8,128)S(1)} %get-tuple-element.13) | data formatting | bytes 1179648
  50.6 0.8 %copy.14 = f32[128,1152]{1,0:T(8,128)} copy(f32[128,1152]{1,0:T(8,128)S(1)} %get-tuple-element.14) | data formatting | bytes 1179648

commit v5 on v4

--- a/solution.py
+++ b/solution.py
@@ -254,9 +254,14 @@
     image_diag = send(10, images.at[2], images.at[3], CORE)
     image_diag_id = send(11, image_ids.at[2], image_ids.at[3], CORE)
     total += tile(2, 0) + tile(2, 1) + tile(2, 2)
+    for copy in report_diag:
+        copy.wait()
+    report_diag_id.wait()
+    total += tile(0, 3) + tile(1, 3) + tile(2, 3)
     image_diag.wait()
     image_diag_id.wait()
-    total += tile(3, 0) + tile(3, 1) + tile(3, 2)
+    total += tile(3, 3)
+
     def report_sum(j):
         out = None
         for i in range(4):
@@ -269,6 +274,13 @@
             out = term if out is None else out + term
         return scale * out
 
+    def image_sum(i):
+        return scale * jnp.dot(
+            coeffs[i],
+            reports[...].reshape(4 * rows, images.shape[2]),
+            preferred_element_type=jnp.float32,
+        )
+
     def coded(number, height, bit):
         slot, first = divmod(number, PIECES)
         lines = pl.ds(first * height, height)
@@ -295,82 +307,66 @@
             22 + step, loss_out.at[step], loss_in.at[step], (CORE, ACROSS, NEAR, FAR)[step]
         )
 
-    across_sum = report_sum(1)
+    across_sum = report_sum(3)
     for k in range(PIECES):
-        put(2 * PIECES + k, across_sum[k * piece : (k + 1) * piece])
-    report_part[1] = report_sum(2)
-    early = reports[:3].reshape(3 * rows, images.shape[2])
-    for i in (3, 2, 1, 0):
-        image_part[i] = scale * jnp.dot(
-            coeffs[i, :, : 3 * rows], early, preferred_element_type=jnp.float32
-        )
-
-    def image_sum(i):
-        return image_part[i] + scale * jnp.dot(
-            coeffs[i, :, 3 * rows :], reports[3], preferred_element_type=jnp.float32
-        )
-
-    for copy in report_diag:
-        copy.wait()
-    report_diag_id.wait()
-    across_second = [coded(2 * PIECES + k, piece, ACROSS) for k in range(2)]
-    for i in range(4):
-        total += tile(i, 3)
+        put(k, across_sum[k * piece : (k + 1) * piece])
+    across_first = [coded(k, piece, ACROSS) for k in range(3)]
+    total += tile(3, 0) + tile(3, 1) + tile(3, 2)
+    image_part[0] = image_sum(3)
+    core_first = send(20, image_part.at[0], core_in.at[0], CORE)
     loss_out[0] = jnp.sum(total.reshape(rows // 8, 8, rows), axis=0)
     loss_copy = loss_step(0)
-    reports_sum = report_sum(3)
+    image_part[2] = image_sum(2)
+    core_first.wait()
+    put(3 * PIECES, image_part[2] + core_in[0])
+    far = coded(3 * PIECES, rows, FAR)
+    report_part[1] = report_sum(2)
+    across_second = []
+    near = []
     for k in range(PIECES):
-        put(k, reports_sum[k * piece : (k + 1) * piece])
-    across_first = [coded(k, piece, ACROSS) for k in range(2)]
-    image_part[3] = image_sum(3)
-    core_first = send(20, image_part.at[3], core_in.at[0], CORE)
-    image_part[2] = image_sum(2)
+        landed = receive(across_first[k], k, piece)
+        if k == 0:
+            across_first.append(coded(3, piece, ACROSS))
+        put(PIECES + k, report_part[1, part(k)] + landed)
+        near.append(coded(PIECES + k, piece, NEAR))
+        if k == 0:
+            across_sum = report_sum(1)
+            for n in range(PIECES):
+                put(2 * PIECES + n, across_sum[n * piece : (n + 1) * piece])
+        else:
+            across_second.append(coded(2 * PIECES + k - 1, piece, ACROSS))
+    across_second.append(coded(3 * PIECES - 1, piece, ACROSS))
+    image_part[1] = image_sum(1)
+    core_second = send(21, image_part.at[1], core_in.at[1], CORE)
     loss_copy.wait()
     loss_out[1] = loss_out[0] + loss_in[0]
     loss_copy = loss_step(1)
-    core_first.wait()
-    put(3 * PIECES, image_part[2] + core_in[0])
-    far = coded(3 * PIECES, rows, FAR)
-    near = []
-    for k in range(PIECES):
-        landed = receive(across_first[k], k, piece)
-        put(PIECES + k, report_part[1, part(k)] + landed)
-        near.append(coded(PIECES + k, piece, NEAR))
-        if k + 2 < PIECES:
-            across_first.append(coded(k + 2, piece, ACROSS))
-        else:
-            across_second.append(coded(2 * PIECES + k, piece, ACROSS))
-        if k == 0:
-            image_part[1] = image_sum(1)
-            core_second = send(21, image_part.at[1], core_in.at[1], CORE)
-        elif k == 1:
-            loss_copy.wait()
-            loss_out[2] = loss_out[1] + loss_in[1]
-            loss_copy = loss_step(2)
-        elif k == 2:
-            own_image = image_sum(0)
-        else:
-            own_report = report_sum(0)
+    own_image = image_sum(0)
+    loss_copy.wait()
+    loss_out[2] = loss_out[1] + loss_in[1]
+    loss_copy = loss_step(2)
+    report_part[0] = report_sum(0)
+    core_second.wait()
+    own_image += core_in[1]
     loss_copy.wait()
     loss_out[3] = loss_out[2] + loss_in[2]
     loss_copy = loss_step(3)
+    for k in range(2):
+        report_part[0, part(k)] += receive(across_second[k], 2 * PIECES + k, piece)
+        report_part[0, part(k)] += receive(near[k], PIECES + k, piece)
 
     def finish(ref, unit_grad):
         norm, unit = normalised(ref)
         return (unit_grad - unit * jnp.sum(unit * unit_grad, axis=1, keepdims=True)) / norm
 
-    core_second.wait()
-    own_image += core_in[1]
     image_grad_ref[...] = finish(image_ref, own_image + receive(far, 3 * PIECES, rows))
     loss_copy.wait()
     pairs = rows * lax.axis_size("blk")
     loss = jnp.sum(loss_out[3] + loss_in[3]) / pairs
     loss_ref[...] = jnp.full(loss_ref.shape, loss, jnp.float32)
-    report_part[0] = own_report
-    for k in range(PIECES):
+    for k in range(2, PIECES):
+        report_part[0, part(k)] += receive(near[k], PIECES + k, piece)
         report_part[0, part(k)] += receive(across_second[k], 2 * PIECES + k, piece)
-    for k in range(PIECES):
-        report_part[0, part(k)] += receive(near[k], PIECES + k, piece)
     report_grad_ref[...] = finish(report_ref, report_part[0])
 
 
@@ -400,7 +396,7 @@
             pltpu.VMEM((4, 8, rows), jnp.int32),
             pltpu.VMEM((4, 8, rows), jnp.int32),
             pltpu.VMEM((4, rows, 4 * rows), jnp.bfloat16),
-            pltpu.VMEM((4, rows, width), f32),
+            pltpu.VMEM((3, rows, width), f32),
             pltpu.VMEM((2, rows, width), f32),
             pltpu.VMEM((2, rows, width), f32),
             pltpu.VMEM((4, rows, width), jnp.int16),

time: 51.6 us -> 51 us (0.988)
    pallas_call x1, Pallas kernels: 47.3 us -> 46.8 us  [kernel_body(): pl.pallas_call(tile_kernel, out_shape=(jax.ShapeDtypeStruct((8, 128), f32...]
where the time goes in v5:
time: 51 us; the launch traced here: 50.9 us
  Pallas kernels  46.8 us (92%)
  local copies, waits for them, and re-layouts  2.14 us (4%)
  between operations  1.93 us (4%)
    pallas_call x1, Pallas kernels, kernel_body(): pl.pallas_call(tile_kernel, out_shape=(jax.ShapeDtypeStruct((8, 128), f32...  46.8 us
    unnamed x2, local copies, waits for them, and re-layouts  1.63 us

profile of v5, /device:TPU:0, one launch (start us, length us, event | category | flops | bytes accessed | tf_op | source)
XLA Modules:
  0.0 50.9 jit_solution(18323154231298634402)
XLA Ops:
  1.9 46.8 %shard_map.85 = (f32[8,128]{1,0:T(8,128)S(1)}, f32[128,1152]{1,0:T(8,128)S(1)}, f32[128,1152]{1,0:T(8,128)S(1)}) custom-call(bf16[128,1152]{1,0:T(8,128)(2,1)} %image_hbm.1, bf16[128,1152]{1,0:T(8,128)(2,1)} %report_hbm.1, s32[1,128]{1,0:T(1,128)} %bitcast.3, s32[1,128]{1,0:T(1,128)} %bitcast.4, f32[1]{0:T(128)S(6)} %copy.11.scale_ref, f32[1]{0:T(128)S(6)} %copy.12.bias_ref), custom_call_target="tpu_custom_call" | custom-call | tf_op jit(solution)/shard_map/pallas_call | solution.py:380
  48.7 0.5 %slice.3 = f32[1,1]{1,0:T(1,128)} slice(f32[8,128]{1,0:T(8,128)S(1)} %get-tuple-element.6), slice={[0:1], [0:1]} | slice | bytes 8 | tf_op jit(solution)/shard_map/slice | solution.py:423
  49.2 0.8 %copy.13 = f32[128,1152]{1,0:T(8,128)} copy(f32[128,1152]{1,0:T(8,128)S(1)} %get-tuple-element.13) | data formatting | bytes 1179648
  50.1 0.8 %copy.14 = f32[128,1152]{1,0:T(8,128)} copy(f32[128,1152]{1,0:T(8,128)S(1)} %get-tuple-element.14) | data formatting | bytes 1179648

commit v6 on v5

--- a/solution.py
+++ b/solution.py
@@ -258,13 +258,9 @@
         copy.wait()
     report_diag_id.wait()
     total += tile(0, 3) + tile(1, 3) + tile(2, 3)
-    image_diag.wait()
-    image_diag_id.wait()
-    total += tile(3, 3)
-
-    def report_sum(j):
+    def report_terms(j, blocks):
         out = None
-        for i in range(4):
+        for i in blocks:
             term = lax.dot_general(
                 coeffs[i, :, j * rows : (j + 1) * rows],
                 images[i],
@@ -274,12 +270,21 @@
             out = term if out is None else out + term
         return scale * out
 
+    def report_sum(j):
+        return report_terms(j, range(4))
+
     def image_sum(i):
         return scale * jnp.dot(
             coeffs[i],
             reports[...].reshape(4 * rows, images.shape[2]),
             preferred_element_type=jnp.float32,
         )
+
+    image_part[2] = image_sum(2)
+    report_part[0] = report_terms(3, range(3))
+    image_diag.wait()
+    image_diag_id.wait()
+    total += tile(3, 3)
 
     def coded(number, height, bit):
         slot, first = divmod(number, PIECES)
@@ -307,7 +312,7 @@
             22 + step, loss_out.at[step], loss_in.at[step], (CORE, ACROSS, NEAR, FAR)[step]
         )
 
-    across_sum = report_sum(3)
+    across_sum = report_part[0] + report_terms(3, (3,))
     for k in range(PIECES):
         put(k, across_sum[k * piece : (k + 1) * piece])
     across_first = [coded(k, piece, ACROSS) for k in range(3)]
@@ -316,11 +321,10 @@
     core_first = send(20, image_part.at[0], core_in.at[0], CORE)
     loss_out[0] = jnp.sum(total.reshape(rows // 8, 8, rows), axis=0)
     loss_copy = loss_step(0)
-    image_part[2] = image_sum(2)
+    report_part[1] = report_sum(2)
     core_first.wait()
     put(3 * PIECES, image_part[2] + core_in[0])
     far = coded(3 * PIECES, rows, FAR)
-    report_part[1] = report_sum(2)
     across_second = []
     near = []
     for k in range(PIECES):
@@ -335,16 +339,16 @@
                 put(2 * PIECES + n, across_sum[n * piece : (n + 1) * piece])
         else:
             across_second.append(coded(2 * PIECES + k - 1, piece, ACROSS))
+        if k == 1 or k == 3:
+            step = k // 2
+            loss_copy.wait()
+            loss_out[step + 1] = loss_out[step] + loss_in[step]
+            loss_copy = loss_step(step + 1)
+        if k == 2:
+            image_part[1] = image_sum(1)
+            core_second = send(21, image_part.at[1], core_in.at[1], CORE)
     across_second.append(coded(3 * PIECES - 1, piece, ACROSS))
-    image_part[1] = image_sum(1)
-    core_second = send(21, image_part.at[1], core_in.at[1], CORE)
-    loss_copy.wait()
-    loss_out[1] = loss_out[0] + loss_in[0]
-    loss_copy = loss_step(1)
     own_image = image_sum(0)
-    loss_copy.wait()
-    loss_out[2] = loss_out[1] + loss_in[1]
-    loss_copy = loss_step(2)
     report_part[0] = report_sum(0)
     core_second.wait()
     own_image += core_in[1]
@@ -360,14 +364,14 @@
         return (unit_grad - unit * jnp.sum(unit * unit_grad, axis=1, keepdims=True)) / norm
 
     image_grad_ref[...] = finish(image_ref, own_image + receive(far, 3 * PIECES, rows))
+    for k in range(2, PIECES):
+        report_part[0, part(k)] += receive(near[k], PIECES + k, piece)
+        report_part[0, part(k)] += receive(across_second[k], 2 * PIECES + k, piece)
+    report_grad_ref[...] = finish(report_ref, report_part[0])
     loss_copy.wait()
     pairs = rows * lax.axis_size("blk")
     loss = jnp.sum(loss_out[3] + loss_in[3]) / pairs
     loss_ref[...] = jnp.full(loss_ref.shape, loss, jnp.float32)
-    for k in range(2, PIECES):
-        report_part[0, part(k)] += receive(near[k], PIECES + k, piece)
-        report_part[0, part(k)] += receive(across_second[k], 2 * PIECES + k, piece)
-    report_grad_ref[...] = finish(report_ref, report_part[0])
 
 
 def kernel_body(image_embed, report_embed, image_study, report_study_index, logit_scale, logit_bias):

time: 51 us -> 50.6 us (level)
  no operation moved by 1% of the time
where the time goes in v6:
time: 50.6 us; the launch traced here: 50.4 us
  Pallas kernels  46.3 us (92%)
  local copies, waits for them, and re-layouts  2.14 us (4%)
  between operations  1.93 us (4%)
    pallas_call x1, Pallas kernels, kernel_body(): pl.pallas_call(tile_kernel, out_shape=(jax.ShapeDtypeStruct((8, 128), f32...  46.3 us
    unnamed x2, local copies, waits for them, and re-layouts  1.63 us

profile of v6, /device:TPU:0, one launch (start us, length us, event | category | flops | bytes accessed | tf_op | source)
XLA Modules:
  0.0 50.4 jit_solution(16646963760777985370)
XLA Ops:
  1.9 46.3 %shard_map.85 = (f32[8,128]{1,0:T(8,128)S(1)}, f32[128,1152]{1,0:T(8,128)S(1)}, f32[128,1152]{1,0:T(8,128)S(1)}) custom-call(bf16[128,1152]{1,0:T(8,128)(2,1)} %image_hbm.1, bf16[128,1152]{1,0:T(8,128)(2,1)} %report_hbm.1, s32[1,128]{1,0:T(1,128)} %bitcast.3, s32[1,128]{1,0:T(1,128)} %bitcast.4, f32[1]{0:T(128)S(6)} %copy.11.scale_ref, f32[1]{0:T(128)S(6)} %copy.12.bias_ref), custom_call_target="tpu_custom_call" | custom-call | tf_op jit(solution)/shard_map/pallas_call | solution.py:384
  48.3 0.5 %slice.3 = f32[1,1]{1,0:T(1,128)} slice(f32[8,128]{1,0:T(8,128)S(1)} %get-tuple-element.6), slice={[0:1], [0:1]} | slice | bytes 8 | tf_op jit(solution)/shard_map/slice | solution.py:427
  48.8 0.8 %copy.13 = f32[128,1152]{1,0:T(8,128)} copy(f32[128,1152]{1,0:T(8,128)S(1)} %get-tuple-element.13) | data formatting | bytes 1179648
  49.6 0.8 %copy.14 = f32[128,1152]{1,0:T(8,128)} copy(f32[128,1152]{1,0:T(8,128)S(1)} %get-tuple-element.14) | data formatting | bytes 1179648

commit v7 on v6

--- a/solution.py
+++ b/solution.py
@@ -151,6 +151,7 @@
     group = lax.axis_index("groups")
     me = lax.axis_index("blk")
     rows = image_ref.shape[0]
+    started = []
     piece = rows // PIECES
 
     def partner(bit):
@@ -167,6 +168,7 @@
             device_id_type=MESH_ID,
         )
         copy.start()
+        started.append(copy)
         return copy
 
     loads = []
@@ -203,12 +205,20 @@
     def near_piece(k):
         return send(32 + k, reports.at[0, part(k)], reports.at[2, part(k)], NEAR)
 
-    report_near = [near_piece(0), near_piece(1)]
+    def across_piece(k):
+        return send(24 + 2 + k, reports.at[0, part(k)], reports.at[1, part(k)], ACROSS)
+
+    def far_piece(k):
+        return send(40 + 8 * PIECES + k, images.at[0, part(k)], images.at[2, part(k)], FAR)
+
+    report_near, report_across, image_far = ([], [], [])
     report_near_id = send(1, report_ids.at[0], report_ids.at[2], NEAR)
-    report_across = send(2, reports.at[0], reports.at[1], ACROSS)
     report_across_id = send(3, report_ids.at[0], report_ids.at[1], ACROSS)
-    image_far = send(4, images.at[0], images.at[2], FAR)
     image_far_id = send(5, image_ids.at[0], image_ids.at[2], FAR)
+    for k in range(PIECES):
+        report_near.append(near_piece(k))
+        image_far.append(far_piece(k))
+        report_across.append(across_piece(k))
     image_core = send(6, images.at[0], images.at[1], CORE)
     image_core_id = send(7, image_ids.at[0], image_ids.at[1], CORE)
 
@@ -232,31 +242,31 @@
         coeffs[i, :, j * rows : (j + 1) * rows] = (-sign * negative).astype(jnp.bfloat16)
         return jnp.maximum(-signed, 0.0) + jnp.log1p(weight)
 
-    image_core.wait()
-    image_core_id.wait()
+    image_core.wait_recv()
+    image_core_id.wait_recv()
     total = tile(0, 0) + tile(1, 0)
-    report_near_id.wait()
+    report_near_id.wait_recv()
     report_diag_id = send(9, report_ids.at[2], report_ids.at[3], ACROSS)
     report_diag = []
     for k in range(PIECES):
-        report_near[k].wait()
-        if k + 2 < PIECES:
-            report_near.append(near_piece(k + 2))
+        report_near[k].wait_recv()
         report_diag.append(
             send(32 + PIECES + k, reports.at[2, part(k)], reports.at[3, part(k)], ACROSS)
         )
     total += tile(0, 2) + tile(1, 2)
-    report_across.wait()
-    report_across_id.wait()
+    for copy in report_across:
+        copy.wait_recv()
+    report_across_id.wait_recv()
     total += tile(0, 1) + tile(1, 1)
-    image_far.wait()
-    image_far_id.wait()
+    for copy in image_far:
+        copy.wait_recv()
+    image_far_id.wait_recv()
     image_diag = send(10, images.at[2], images.at[3], CORE)
     image_diag_id = send(11, image_ids.at[2], image_ids.at[3], CORE)
     total += tile(2, 0) + tile(2, 1) + tile(2, 2)
     for copy in report_diag:
-        copy.wait()
-    report_diag_id.wait()
+        copy.wait_recv()
+    report_diag_id.wait_recv()
     total += tile(0, 3) + tile(1, 3) + tile(2, 3)
     def report_terms(j, blocks):
         out = None
@@ -282,8 +292,8 @@
 
     image_part[2] = image_sum(2)
     report_part[0] = report_terms(3, range(3))
-    image_diag.wait()
-    image_diag_id.wait()
+    image_diag.wait_recv()
+    image_diag_id.wait_recv()
     total += tile(3, 3)
 
     def coded(number, height, bit):
@@ -304,7 +314,7 @@
     def receive(copies, number, height):
         slot, first = divmod(number, PIECES)
         for copy in copies:
-            copy.wait()
+            copy.wait_recv()
         return decode(codes_in.at[slot, pl.ds(first * height, height)], steps_in.at[number])
 
     def loss_step(step):
@@ -322,7 +332,7 @@
     loss_out[0] = jnp.sum(total.reshape(rows // 8, 8, rows), axis=0)
     loss_copy = loss_step(0)
     report_part[1] = report_sum(2)
-    core_first.wait()
+    core_first.wait_recv()
     put(3 * PIECES, image_part[2] + core_in[0])
     far = coded(3 * PIECES, rows, FAR)
     across_second = []
@@ -341,7 +351,7 @@
             across_second.append(coded(2 * PIECES + k - 1, piece, ACROSS))
         if k == 1 or k == 3:
             step = k // 2
-            loss_copy.wait()
+            loss_copy.wait_recv()
             loss_out[step + 1] = loss_out[step] + loss_in[step]
             loss_copy = loss_step(step + 1)
         if k == 2:
@@ -350,9 +360,9 @@
     across_second.append(coded(3 * PIECES - 1, piece, ACROSS))
     own_image = image_sum(0)
     report_part[0] = report_sum(0)
-    core_second.wait()
+    core_second.wait_recv()
     own_image += core_in[1]
-    loss_copy.wait()
+    loss_copy.wait_recv()
     loss_out[3] = loss_out[2] + loss_in[2]
     loss_copy = loss_step(3)
     for k in range(2):
@@ -368,10 +378,12 @@
         report_part[0, part(k)] += receive(near[k], PIECES + k, piece)
         report_part[0, part(k)] += receive(across_second[k], 2 * PIECES + k, piece)
     report_grad_ref[...] = finish(report_ref, report_part[0])
-    loss_copy.wait()
+    loss_copy.wait_recv()
     pairs = rows * lax.axis_size("blk")
     loss = jnp.sum(loss_out[3] + loss_in[3]) / pairs
     loss_ref[...] = jnp.full(loss_ref.shape, loss, jnp.float32)
+    for copy in started:
+        copy.wait_send()
 
 
 def kernel_body(image_embed, report_embed, image_study, report_study_index, logit_scale, logit_bias):
@@ -410,8 +422,8 @@
             pltpu.VMEM((4, 8, rows), f32),
             pltpu.VMEM((4, 8, rows), f32),
             pltpu.SemaphoreType.DMA((4,)),
-            pltpu.SemaphoreType.DMA((40 + 8 * PIECES,)),
-            pltpu.SemaphoreType.DMA((40 + 8 * PIECES,)),
+            pltpu.SemaphoreType.DMA((40 + 9 * PIECES,)),
+            pltpu.SemaphoreType.DMA((40 + 9 * PIECES,)),
         ],
         compiler_params=pltpu.CompilerParams(
             collective_id=0, has_side_effects=True, vmem_limit_bytes=48 * 1024 * 1024

time: 50.6 us -> 49.1 us (0.970)
  Pallas kernels: 46.3 us -> 44.9 us
    pallas_call x1, Pallas kernels: 46.3 us -> 44.9 us  [kernel_body(): pl.pallas_call(tile_kernel, out_shape=(jax.ShapeDtypeStruct((8, 128), f32...]
where the time goes in v7:
time: 49.1 us; the launch traced here: 49 us
  Pallas kernels  44.9 us (91%)
  local copies, waits for them, and re-layouts  2.14 us (4%)
  between operations  1.93 us (4%)
    pallas_call x1, Pallas kernels, kernel_body(): pl.pallas_call(tile_kernel, out_shape=(jax.ShapeDtypeStruct((8, 128), f32...  44.9 us
    unnamed x2, local copies, waits for them, and re-layouts  1.63 us

profile of v7, /device:TPU:0, one launch (start us, length us, event | category | flops | bytes accessed | tf_op | source)
XLA Modules:
  0.0 49.0 jit_solution(9180196027956594422)
XLA Ops:
  1.9 44.9 %shard_map.85 = (f32[8,128]{1,0:T(8,128)S(1)}, f32[128,1152]{1,0:T(8,128)S(1)}, f32[128,1152]{1,0:T(8,128)S(1)}) custom-call(bf16[128,1152]{1,0:T(8,128)(2,1)} %image_hbm.1, bf16[128,1152]{1,0:T(8,128)(2,1)} %report_hbm.1, s32[1,128]{1,0:T(1,128)} %bitcast.3, s32[1,128]{1,0:T(1,128)} %bitcast.4, f32[1]{0:T(128)S(6)} %copy.11.scale_ref, f32[1]{0:T(128)S(6)} %copy.12.bias_ref), custom_call_target="tpu_custom_call" | custom-call | tf_op jit(solution)/shard_map/pallas_call | solution.py:396
  46.8 0.5 %slice.3 = f32[1,1]{1,0:T(1,128)} slice(f32[8,128]{1,0:T(8,128)S(1)} %get-tuple-element.6), slice={[0:1], [0:1]} | slice | bytes 8 | tf_op jit(solution)/shard_map/slice | solution.py:439
  47.3 0.8 %copy.13 = f32[128,1152]{1,0:T(8,128)} copy(f32[128,1152]{1,0:T(8,128)S(1)} %get-tuple-element.13) | data formatting | bytes 1179648
  48.2 0.8 %copy.14 = f32[128,1152]{1,0:T(8,128)} copy(f32[128,1152]{1,0:T(8,128)S(1)} %get-tuple-element.14) | data formatting | bytes 1179648
